TPU v7x, 128 devices: a whole 4x4x4 slice. The times are simulated.
128 devices in a mesh: row: 16 (over x, z_lo, core), col: 8 (over z_hi, y).
Axes of the slice: x: 4, y: 4, z: 4 (z_hi: 2, z_lo: 2; z = z_hi * 2 + z_lo), core: 2. Of those that a mesh axis runs over, the one named last changes fastest.
Arguments:
- surface: float32 [16, 2048, 2048], P(None, 'row', 'col'), may hold values from -6 to 6
- coupling: float32 [3, 2048, 2048], P(None, 'row', 'col'), may hold values from 0.1 to 1
- w_stencil: float32 [3, 9, 16, 16], replicated, may hold values from -0.5 to 0.5
- w_patch: bfloat16 [4096, 256], replicated, may hold values from -0.09375 to 0.09375
- w_query: bfloat16 [2, 256, 256], replicated, as said below
- w_key: bfloat16 [2, 256, 256], replicated, as said below
- w_value: bfloat16 [2, 256, 256], replicated, may hold values from -0.375 to 0.375
- w_out: bfloat16 [2, 256, 256], replicated, may hold values from -4 to 4
- w_unpatch: bfloat16 [256, 4096], replicated, may hold values from -0.375 to 0.375
Outputs:
- section: float32 [16, 2048, 2048], P(None, 'row', 'col')
Inputs may be any that keep to these rules, and one draw needn't show every extreme that they name: `w_key`: key projections: normal entries times 256^-0.5. `w_query`: query projections.
All inputs are finite; a program needn't handle non-finite values.
Results may differ from a plain program's by a relative error of at most 0.035.
Values may be sent and summed in bfloat16 or wider, within the bound.
A program may use at most 128 MiB of HBM per device.

v0:
```python
import jax
import jax.numpy as jnp
from jax import lax
from jax.sharding import PartitionSpec as P

C = 16
E = 256
H = 8
PATCH = 16
LAYERS = 3


def with_halo(block, sides, width):
    for axis, dim in sides:
        count = lax.axis_size(axis)
        forward = [(i, i + 1) for i in range(count - 1)]
        backward = [(target, source) for source, target in forward]
        low = lax.ppermute(
            lax.slice_in_dim(block, block.shape[dim] - width, None, axis=dim), axis, forward
        )
        high = lax.ppermute(lax.slice_in_dim(block, 0, width, axis=dim), axis, backward)
        block = jnp.concatenate([low, block, high], axis=dim)
    return block


def advance(padded, coefficient, weights):
    row_count = padded.shape[1] - 2
    col_count = padded.shape[2] - 2
    summed = jnp.zeros((padded.shape[0], row_count, col_count), jnp.float32)
    for index in range(9):
        shift_r = index // 3
        shift_c = index % 3
        summed = summed + jnp.einsum(
            "dc,cxy->dxy",
            weights[index],
            padded[:, shift_r : shift_r + row_count, shift_c : shift_c + col_count],
            precision=lax.Precision.HIGHEST,
        )
    return padded[:, 1:-1, 1:-1] + coefficient * jnp.tanh(summed)


def patchify(fine, leading, trailing):
    channels = fine.shape[0]
    return (
        fine.reshape(channels, leading, PATCH, trailing, PATCH)
        .transpose(1, 3, 0, 2, 4)
        .reshape(leading * trailing, -1)
    )


def unpatchify(detail, leading, trailing):
    return (
        detail.reshape(leading, trailing, C, PATCH, PATCH)
        .transpose(2, 0, 3, 1, 4)
        .reshape(C, leading * PATCH, trailing * PATCH)
    )


def normed(coarse):
    return (coarse * lax.rsqrt(jnp.mean(coarse * coarse, axis=-1, keepdims=True) + 1e-06)).astype(
        jnp.bfloat16
    )


def arrange(matrix, leading, trailing, layout_order):
    dims = (leading, trailing, H, E // H)
    moved = matrix.reshape(dims).transpose(layout_order)
    return moved.reshape(moved.shape[0] * moved.shape[1], moved.shape[2] * moved.shape[3])


def restore(mixed, leading, trailing, layout_order):
    dims = (leading, trailing, H, E // H)
    shaped = mixed.reshape(tuple((dims[place] for place in layout_order)))
    inverse = tuple((layout_order.index(place) for place in range(4)))
    return shaped.transpose(inverse).reshape(leading * trailing, E)


def attend(queries, lookups, values):
    head_size = E // H
    item_count = queries.shape[0]
    query_set = queries.reshape(item_count, -1, head_size)
    lookup_set = lookups.reshape(item_count, -1, head_size)
    value_set = values.reshape(item_count, -1, head_size)
    scores = jnp.einsum(
        "nid,njd->nij", query_set, lookup_set, preferred_element_type=jnp.float32
    ) * head_size ** (-0.5)
    weights = jax.nn.softmax(scores, axis=-1).astype(jnp.bfloat16)
    mixed = jnp.einsum(
        "nij,njd->nid", weights, value_set, preferred_element_type=jnp.float32
    ).astype(jnp.bfloat16)
    return mixed.reshape(item_count, -1)


def attend_items(triple):
    return attend(triple[0][0], triple[1][0], triple[2][0])[None]


def along_rows(queries, lookups, values):
    parts = lax.axis_size("col")
    width = queries.shape[1]
    moved = attend_items(
        (
            lax.all_to_all(
                queries.reshape(parts, -1, width), "col", split_axis=0, concat_axis=2, tiled=True
            ),
            lax.all_to_all(
                lookups.reshape(parts, -1, width), "col", split_axis=0, concat_axis=2, tiled=True
            ),
            lax.all_to_all(
                values.reshape(parts, -1, width), "col", split_axis=0, concat_axis=2, tiled=True
            ),
        )
    )
    returned = lax.all_to_all(moved, "col", split_axis=2, concat_axis=0, tiled=True)
    return returned.reshape(queries.shape)


def along_cols(queries, lookups, values):
    parts = lax.axis_size("row")
    width = queries.shape[1]
    moved = attend_items(
        (
            lax.all_to_all(
                queries.reshape(parts, -1, width), "row", split_axis=0, concat_axis=2, tiled=True
            ),
            lax.all_to_all(
                lookups.reshape(parts, -1, width), "row", split_axis=0, concat_axis=2, tiled=True
            ),
            lax.all_to_all(
                values.reshape(parts, -1, width), "row", split_axis=0, concat_axis=2, tiled=True
            ),
        )
    )
    returned = lax.all_to_all(moved, "row", split_axis=2, concat_axis=0, tiled=True)
    return returned.reshape(queries.shape)


def axial(coarse, leading, trailing, layout_order, w_q, w_k, w_v, w_o, transport):
    normal_in = normed(coarse)
    queries = arrange(
        jnp.dot(normal_in, w_q, preferred_element_type=jnp.float32).astype(jnp.bfloat16),
        leading,
        trailing,
        layout_order,
    )
    lookups = arrange(
        jnp.dot(normal_in, w_k, preferred_element_type=jnp.float32).astype(jnp.bfloat16),
        leading,
        trailing,
        layout_order,
    )
    values = arrange(
        jnp.dot(normal_in, w_v, preferred_element_type=jnp.float32).astype(jnp.bfloat16),
        leading,
        trailing,
        layout_order,
    )
    mixed = restore(transport(queries, lookups, values), leading, trailing, layout_order)
    return coarse + jnp.dot(mixed, w_o, preferred_element_type=jnp.float32)


def on_device(surface, coupling, w_stencil, w_patch, w_query, w_key, w_value, w_out, w_unpatch):
    tile_rows = surface.shape[1]
    tile_cols = surface.shape[2]
    state = surface
    for layer in range(LAYERS):
        padded = with_halo(state, (("row", 1), ("col", 2)), 1)
        state = advance(padded, coupling[layer], w_stencil[layer])
    patch_rows = tile_rows // PATCH
    patch_cols = tile_cols // PATCH
    coarse = jnp.dot(
        patchify(state.astype(jnp.bfloat16), patch_rows, patch_cols),
        w_patch,
        preferred_element_type=jnp.float32,
    )
    coarse = axial(
        coarse,
        patch_rows,
        patch_cols,
        (0, 2, 1, 3),
        w_query[0],
        w_key[0],
        w_value[0],
        w_out[0],
        along_rows,
    )
    coarse = axial(
        coarse,
        patch_rows,
        patch_cols,
        (1, 2, 0, 3),
        w_query[1],
        w_key[1],
        w_value[1],
        w_out[1],
        along_cols,
    )
    detail = jnp.dot(coarse.astype(jnp.bfloat16), w_unpatch, preferred_element_type=jnp.float32)
    return state + unpatchify(detail, patch_rows, patch_cols)


def solution(mesh):
    in_specs = (P(None, "row", "col"), P(None, "row", "col"), P(), P(), P(), P(), P(), P(), P())
    out_specs = P(None, "row", "col")
    return jax.shard_map(
        on_device, mesh=mesh, in_specs=in_specs, out_specs=out_specs, check_vma=False
    )
```

profile of v0, /device:TPU:1, one launch (start us, length us, event | category | flops | bytes accessed | tf_op | source)
XLA Modules:
  0.0 442.8 jit_solution(17316147162542466090)
XLA Ops:
  3.0 4.9 %collective-permute-start = (f32[16,1,256]{2,0,1:T(8,128)S(1)}, f32[16,1,256]{2,0,1:T(8,128)S(1)}, u32[]{:S(2)}, u32[]{:S(2)}) collective-permute-start(f32[16,1,256]{2,0,1:T(8,128)S(1)} %get-tuple-element.19), channel_id=1, source_target_pairs={{0,8},{8,16},{16,24},{24,32},{32,40},{40,48},{48,56},{56,64},{64,7... | collective-permute-start | bytes 49160 | tf_op jit(solution)/shard_map/ppermute | solution.py:18
  10.0 4.9 %fusion.125 = f32[16,128,256]{2,0,1:T(8,128)} fusion(f32[3,9,16,16]{3,2,1,0:T(8,128)} %param.11, f32[16,128,256]{2,1,0:T(8,128)S(1)} %copy-done.10), kind=kOutput, calls=%fused_computation.168 | convolution fusion | flops 100663296 | bytes 4202496 | tf_op jit(solution)/shard_map/dc,cxy->dxy/dot_general | solution.py:33
  22.2 3.9 collective-permute-start.2
  27.9 4.9 %fusion.6 = f32[128,256,16]{1,2,0:T(8,128)} fusion(f32[16,1,256]{2,0,1:T(8,128)} %copy-done.31, f32[16,128,256]{2,0,1:T(8,128)} %copy-done.12, f32[3,9,16,16]{3,2,1,0:T(8,128)} %param.11), kind=kOutput, calls=%fused_computation.22 | convolution fusion | flops 101191680 | bytes 4218880 | tf_op jit(solution)/shard_map/dc,cxy->dxy/dot_general | solution.py:33
  32.8 4.0 fusion.2
  38.3 5.2 %fusion.36 = f32[128,256,16]{1,2,0:T(8,128)} fusion(f32[16,130,256]{2,0,1:T(8,128)} %copy-done.1, f32[16,130,1]{2,0,1:T(8,128)S(1)} %copy.141, f32[3,9,16,16]{3,2,1,0:T(8,128)} %param.11), kind=kOutput, calls=%fused_computation.49 | convolution fusion | flops 101187584 | bytes 4243584 | tf_op jit(solution)/shard_map/dc,cxy->dxy/dot_general | solution.py:33
  43.6 4.2 fusion.64
  47.7 4.2 fusion.33
  53.4 4.3 fusion.30
  61.1 8.1 %fusion.68 = f32[16,128,256]{2,0,1:T(8,128)S(1)} fusion(f32[128,256,16]{1,2,0:T(8,128)S(1)} %copy-done.15, f32[128,256,16]{1,2,0:T(8,128)} %fusion.64, f32[128,256,16]{1,2,0:T(8,128)S(1)} %fusion.27, f32[16,128,256]{2,0,1:T(8,128)S(1)} %copy-done.14, f32[128,256,16]{1,2,0:T(8,128)} %fusion.33, f32[128,256,16]{1,2,0:T(8,128)S(1)} %fusion.30, ...), kind=kOutput, calls=%fused_computation.85 | convolution fusion | flops 106430464 | bytes 23249024 | tf_op jit(solution)/shard_map/dc,cxy->dxy/dot_general | solution.py:33
  69.3 3.9 collective-permute-start.4
  75.2 4.0 fusion.115
  83.2 4.4 collective-permute-start.6
  88.9 4.8 %fusion.14 = f32[128,256,16]{1,2,0:T(8,128)} fusion(f32[16,1,256]{2,0,1:T(8,128)S(1)} %collective-permute-done.5, f32[16,128,256]{2,0,1:T(8,128)} %copy-done.4, f32[3,9,16,16]{3,2,1,0:T(8,128)} %param.11), kind=kOutput, calls=%fused_computation.30 | convolution fusion | flops 101191680 | bytes 4218880 | tf_op jit(solution)/shard_map/dc,cxy->dxy/dot_general | solution.py:33
  93.8 4.0 fusion.10
  100.2 3.7 pad_maximum_fusion
  117.8 4.2 bitcast_add_fusion.1
  122.1 3.9 collective-permute-start.8
  127.9 4.0 fusion.101
  136.0 4.4 collective-permute-start.10
  141.7 4.8 %fusion.22 = f32[128,256,16]{1,2,0:T(8,128)} fusion(f32[16,1,256]{2,0,1:T(8,128)S(1)} %collective-permute-done.9, f32[16,128,256]{2,0,1:T(8,128)} %copy-done.7, f32[3,9,16,16]{3,2,1,0:T(8,128)} %param.11), kind=kOutput, calls=%fused_computation.38 | convolution fusion | flops 101191680 | bytes 4218880 | tf_op jit(solution)/shard_map/dc,cxy->dxy/dot_general | solution.py:33
  146.5 4.0 fusion.18
  170.4 5.9 %fusion.181 = (bf16[16,128,256]{2,0,1:T(8,128)(2,1)S(1)}, f32[16,128,256]{2,0,1:T(8,128)}) fusion(f32[16,128,256]{2,0,1:T(8,128)S(1)} %copy-done.9, f32[3,9,16,16]{3,2,1,0:T(8,128)} %param.11, f32[16,130,257]{2,0,1:T(8,128)S(1)} %get-tuple-element.5, f32[128,256,16]{1,2,0:T(8,128)S(1)} %copy-done.19, f32[128,256,16]{1,2,0:T(8,128)S(1)} %fusion.40, ...), kind=kOutput, calls=%fused_computation.226 | convolution fusion | flops 106430464 | bytes 24256512 | tf_op jit(solution)/shard_map/dc,cxy->dxy/dot_general | solution.py:33
  176.3 7.6 %reshape.118 = bf16[16,8,16,16,16]{4,3,0,2,1:T(8,128)(2,1)} reshape(bf16[16,128,256]{2,0,1:T(8,128)(2,1)S(1)} %get-tuple-element.24) | data formatting | bytes 2097152 | tf_op jit(solution)/shard_map/reshape | solution.py:45
  183.8 12.6 %copy.214 = bf16[16,8,16,16,16]{4,2,0,3,1:T(8,128)(2,1)} copy(bf16[16,8,16,16,16]{4,3,0,2,1:T(8,128)(2,1)} %reshape.118) | data formatting | bytes 2097152 | tf_op jit(solution)/shard_map/reshape | solution.py:45
  196.4 15.1 %reshape.119 = bf16[128,4096]{1,0:T(8,128)(2,1)S(1)} reshape(bf16[8,16,16,16,16]{4,3,2,1,0:T(8,128)(2,1)} %bitcast.338) | data formatting | bytes 2097152 | tf_op jit(solution)/shard_map/reshape | solution.py:47
  215.1 15.7 %all-to-all-start = ((bf16[8,8,512]{2,1,0:T(8,128)(2,1)}), bf16[8,8,512]{2,1,0:T(8,128)(2,1)S(1)}, u32[]{:S(2)}, u32[]{:S(2)}) async-start(bf16[8,8,512]{2,1,0:T(8,128)(2,1)} %reshape_reshape.24), calls=%async_computation | async-start | bytes 131072 | tf_op jit(solution)/shard_map/all_to_all | solution.py:103
  232.0 5.5 %all-to-all-done = bf16[8,8,512]{2,1,0:T(8,128)(2,1)S(1)} async-done(((bf16[8,8,512]{2,1,0:T(8,128)(2,1)}), bf16[8,8,512]{2,1,0:T(8,128)(2,1)S(1)}, u32[]{:S(2)}, u32[]{:S(2)}) %all-to-all-start) | async-done | bytes 65568 | tf_op jit(solution)/shard_map/all_to_all | solution.py:103
  242.3 5.6 %all-to-all-done.1 = bf16[8,8,512]{2,1,0:T(8,128)(2,1)S(1)} async-done(((bf16[8,8,512]{2,1,0:T(8,128)(2,1)}), bf16[8,8,512]{2,1,0:T(8,128)(2,1)S(1)}, u32[]{:S(2)}, u32[]{:S(2)}) %all-to-all-start.1) | async-done | bytes 65568 | tf_op jit(solution)/shard_map/all_to_all | solution.py:106
  252.4 5.7 %all-to-all-done.2 = bf16[8,8,512]{2,1,0:T(8,128)(2,1)S(1)} async-done(((bf16[8,8,512]{2,1,0:T(8,128)(2,1)}), bf16[8,8,512]{2,1,0:T(8,128)(2,1)S(1)}, u32[]{:S(2)}, u32[]{:S(2)}) %all-to-all-start.2) | async-done | bytes 65568 | tf_op jit(solution)/shard_map/all_to_all | solution.py:109
  259.0 3.8 copy.168
  263.5 23.5 %reduce = bf16[4096,8]{1,0:T(8,128)(2,1)S(1)} reduce(bf16[4096,1,8]{2,1,0:T(2,128)(2,1)} %bitcast.339, bf16[]{:T(256)} %broadcast.57), dimensions={1}, to_apply=%bitcast.292.reduce_sub_computation | reduce | bytes 131074
  288.0 9.1 %all_to_all.120 = bf16[8,2,2048]{2,1,0:T(2,128)(2,1)S(1)} all-to-all(bf16[8,2,2048]{2,1,0:T(2,128)(2,1)S(1)} %reshape.157), channel_id=1, replica_groups=mesh['row'=16,'col'=8] {'col'}, dimensions={0} | all-to-all | bytes 131072 | tf_op jit(solution)/shard_map/all_to_all | solution.py:114
  297.1 4.5 %reshape.158 = bf16[4096,1,8]{2,1,0:T(2,128)(2,1)} reshape(bf16[8,2,2048]{2,1,0:T(2,128)(2,1)S(1)} %all_to_all.120) | data formatting | bytes 131072
  301.7 4.4 copy.169
  309.3 12.5 %all-to-all-start.4 = ((bf16[16,8,256]{2,1,0:T(8,128)(2,1)}), bf16[16,8,256]{2,1,0:T(8,128)(2,1)S(1)}, u32[]{:S(2)}, u32[]{:S(2)}) async-start(bf16[16,8,256]{2,1,0:T(8,128)(2,1)} %reshape_reshape.28), calls=%async_computation.4 | async-start | bytes 131072 | tf_op jit(solution)/shard_map/all_to_all | solution.py:123
  324.0 3.6 all-to-all-done.4
  327.6 3.7 all-to-all-start.5
  337.2 4.0 all-to-all-start.6
  342.0 4.9 %all-to-all-done.6 = bf16[16,8,256]{2,1,0:T(8,128)(2,1)S(1)} async-done(((bf16[16,8,256]{2,1,0:T(8,128)(2,1)}), bf16[16,8,256]{2,1,0:T(8,128)(2,1)S(1)}, u32[]{:S(2)}, u32[]{:S(2)}) %all-to-all-start.6) | async-done | bytes 65568 | tf_op jit(solution)/shard_map/all_to_all | solution.py:129
  347.9 3.8 copy.183
  351.7 23.5 %reduce.1 = bf16[4096,8]{1,0:T(8,128)(2,1)S(1)} reduce(bf16[4096,1,8]{2,1,0:T(2,128)(2,1)} %bitcast.340, bf16[]{:T(256)} %broadcast.57), dimensions={1}, to_apply=%bitcast.294.reduce_sub_computation | reduce | bytes 131074
  376.3 9.0 %all_to_all.121 = bf16[16,2,1024]{2,1,0:T(2,128)(2,1)S(1)} all-to-all(bf16[16,2,1024]{2,1,0:T(2,128)(2,1)S(1)} %reshape.159), channel_id=1, replica_groups=mesh['row'=16,'col'=8] {'row'}, dimensions={0} | all-to-all | bytes 131072 | tf_op jit(solution)/shard_map/all_to_all | solution.py:134
  385.3 4.5 %reshape.160 = bf16[4096,1,8]{2,1,0:T(2,128)(2,1)} reshape(bf16[16,2,1024]{2,1,0:T(2,128)(2,1)S(1)} %all_to_all.121) | data formatting | bytes 131072
  389.8 4.4 copy.184
  396.6 10.4 %reshape.128 = f32[8,16,16,16,16]{4,3,2,1,0:T(8,128)} reshape(f32[128,4096]{1,0:T(8,128)} %fusion.74) | data formatting | bytes 4194304 | tf_op jit(solution)/shard_map/reshape | solution.py:53
  407.1 17.7 %copy.213 = f32[8,16,16,16,16]{4,1,2,3,0:T(8,128)} copy(f32[8,16,16,16,16]{4,3,2,1,0:T(8,128)} %reshape.128) | data formatting | bytes 4194304 | tf_op jit(solution)/shard_map/reshape | solution.py:53
  424.8 12.5 %reshape.129 = f32[16,128,256]{2,0,1:T(8,128)} reshape(f32[16,8,16,16,16]{4,3,0,2,1:T(8,128)} %bitcast.337) | data formatting | bytes 4194304 | tf_op jit(solution)/shard_map/reshape | solution.py:55
  (190 shorter events, 109.0 us)
Async XLA Ops:
  0.0 394.7 %copy-start = (bf16[256,4096]{1,0:T(8,128)(2,1)S(1)}, bf16[256,4096]{1,0:T(8,128)(2,1)}, u32[]{:S(2)}) copy-start(bf16[256,4096]{1,0:T(8,128)(2,1)} %param.17) | copy-start | bytes 6291460
  0.0 10.0 %copy-start.10 = (f32[16,128,256]{2,1,0:T(8,128)S(1)}, f32[16,128,256]{2,1,0:T(8,128)}, u32[]{:S(2)}) copy-start(f32[16,128,256]{2,1,0:T(8,128)} %param.9) | copy-start | bytes 6291460
  3.0 11.9 %copy-start.12 = (f32[16,128,256]{2,0,1:T(8,128)}, f32[16,128,256]{2,0,1:T(8,128)S(1)}, u32[]{:S(2)}) copy-start(f32[16,128,256]{2,0,1:T(8,128)S(1)} %copy.147) | copy-start | bytes 6291460
  3.0 11.9 %collective-permute-start = (f32[16,1,256]{2,0,1:T(8,128)S(1)}, f32[16,1,256]{2,0,1:T(8,128)S(1)}, u32[]{:S(2)}, u32[]{:S(2)}) collective-permute-start(f32[16,1,256]{2,0,1:T(8,128)S(1)} %get-tuple-element.19), channel_id=1, source_target_pairs={{0,8},{8,16},{16,24},{24,32},{32,40},{40,48},{48,56},{56,64},{64,7... | collective-permute-start | bytes 49160 | tf_op jit(solution)/shard_map/ppermute | solution.py:18
  7.9 7.0 %copy-start.23 = (f32[3,128,256]{2,1,0:T(8,128)S(1)}, f32[3,128,256]{2,1,0:T(8,128)}, u32[]{:S(2)}) copy-start(f32[3,128,256]{2,1,0:T(8,128)} %param.10) | copy-start | bytes 1179652
  8.0 8.8 %collective-permute-start.1 = (f32[16,1,256]{2,0,1:T(8,128)S(1)}, f32[16,1,256]{2,0,1:T(8,128)S(1)}, u32[]{:S(2)}, u32[]{:S(2)}) collective-permute-start(f32[16,1,256]{2,0,1:T(8,128)S(1)} %get-tuple-element.20), channel_id=1, source_target_pairs={{8,0},{16,8},{24,16},{32,24},{40,32},{48,40},{56,48},{64,56},{72,6... | collective-permute-start | bytes 49160 | tf_op jit(solution)/shard_map/ppermute | solution.py:21
  16.8 1.7 copy-start.1
  22.2 10.6 %copy-start.13 = (f32[16,128,256]{2,0,1:T(8,128)S(1)}, f32[16,128,256]{2,0,1:T(8,128)}, u32[]{:S(2)}) copy-start(f32[16,128,256]{2,0,1:T(8,128)} %copy-done.12) | copy-start | bytes 6291460
  22.2 10.6 %copy-start.30 = (f32[16,1,256]{2,0,1:T(8,128)S(1)}, f32[16,1,256]{2,0,1:T(8,128)}, u32[]{:S(2)}) copy-start(f32[16,1,256]{2,0,1:T(8,128)} %copy-done.29) | copy-start | bytes 49156
  22.2 14.6 %collective-permute-start.2 = (f32[16,130,1]{1,0,2:T(8,128)}, f32[16,130,1]{1,0,2:T(8,128)}, u32[]{:S(2)}, u32[]{:S(2)}) collective-permute-start(f32[16,130,1]{1,0,2:T(8,128)} %copy.140), channel_id=1, source_target_pairs={{0,1},{1,2},{2,3},{3,4},{4,5},{5,6},{6,7},{8,9},{9,10},{10,11},{11... | collective-permute-start | bytes 24968 | tf_op jit(solution)/shard_map/ppermute | solution.py:18
  26.1 25.8 %collective-permute-start.3 = (f32[16,130,1]{1,0,2:T(8,128)}, f32[16,130,1]{1,0,2:T(8,128)}, u32[]{:S(2)}, u32[]{:S(2)}) collective-permute-start(f32[16,130,1]{1,0,2:T(8,128)} %copy.143), channel_id=1, source_target_pairs={{1,0},{2,1},{3,2},{4,3},{5,4},{6,5},{7,6},{9,8},{10,9},{11,10},{12... | collective-permute-start | bytes 24968 | tf_op jit(solution)/shard_map/ppermute | solution.py:21
  38.3 5.3 %copy-start.2 = (f32[16,130,256]{2,0,1:T(8,128)S(1)}, f32[16,130,256]{2,0,1:T(8,128)}, u32[]{:S(2)}) copy-start(f32[16,130,256]{2,0,1:T(8,128)} %copy-done.1) | copy-start | bytes 6389764
  53.4 4.4 copy-start.3
  53.4 7.7 %copy-start.15 = (f32[128,256,16]{1,2,0:T(8,128)S(1)}, f32[128,256,16]{1,2,0:T(8,128)}, u32[]{:S(2)}) copy-start(f32[128,256,16]{1,2,0:T(8,128)} %fusion.6) | copy-start | bytes 6291460
  53.4 7.7 %copy-start.16 = (f32[128,256,16]{1,2,0:T(8,128)S(1)}, f32[128,256,16]{1,2,0:T(8,128)}, u32[]{:S(2)}) copy-start(f32[128,256,16]{1,2,0:T(8,128)} %fusion.2) | copy-start | bytes 6291460
  57.8 3.3 copy-start.11
  57.8 3.3 copy-start.14
  69.3 9.9 %copy-start.4 = (f32[16,128,256]{2,0,1:T(8,128)}, f32[16,128,256]{2,0,1:T(8,128)S(1)}, u32[]{:S(2)}) copy-start(f32[16,128,256]{2,0,1:T(8,128)S(1)} %fusion.68) | copy-start | bytes 6291460
  69.3 9.8 %collective-permute-start.4 = (f32[16,1,256]{2,0,1:T(8,128)S(1)}, f32[16,1,256]{2,0,1:T(8,128)S(1)}, u32[]{:S(2)}, u32[]{:S(2)}) collective-permute-start(f32[16,1,256]{2,0,1:T(8,128)S(1)} %get-tuple-element.17), channel_id=1, source_target_pairs={{0,8},{8,16},{16,24},{24,32},{32,40},{40,48},{48,56},{56,64},{64,7... | collective-permute-start | bytes 49160 | tf_op jit(solution)/shard_map/ppermute | solution.py:18
  73.2 5.9 %collective-permute-start.5 = (f32[16,1,256]{2,0,1:T(8,128)S(1)}, f32[16,1,256]{2,0,1:T(8,128)S(1)}, u32[]{:S(2)}, u32[]{:S(2)}) collective-permute-start(f32[16,1,256]{2,0,1:T(8,128)S(1)} %get-tuple-element.18), channel_id=1, source_target_pairs={{8,0},{16,8},{24,16},{32,24},{40,32},{48,40},{56,48},{64,56},{72,6... | collective-permute-start | bytes 49160 | tf_op jit(solution)/shard_map/ppermute | solution.py:21
  83.2 10.6 %copy-start.5 = (f32[16,128,256]{2,0,1:T(8,128)S(1)}, f32[16,128,256]{2,0,1:T(8,128)}, u32[]{:S(2)}) copy-start(f32[16,128,256]{2,0,1:T(8,128)} %copy-done.4) | copy-start | bytes 6291460
  83.2 15.3 %collective-permute-start.6 = (f32[16,130,1]{1,0,2:T(8,128)S(1)}, f32[16,130,1]{1,0,2:T(8,128)S(1)}, u32[]{:S(2)}, u32[]{:S(2)}) collective-permute-start(f32[16,130,1]{1,0,2:T(8,128)S(1)} %copy.148), channel_id=1, source_target_pairs={{0,1},{1,2},{2,3},{3,4},{4,5},{5,6},{6,7},{8,9},{9,10},{10,11},{11... | collective-permute-start | bytes 24968 | tf_op jit(solution)/shard_map/ppermute | solution.py:18
  87.6 10.1 %collective-permute-start.7 = (f32[16,130,1]{1,0,2:T(8,128)S(1)}, f32[16,130,1]{1,0,2:T(8,128)S(1)}, u32[]{:S(2)}, u32[]{:S(2)}) collective-permute-start(f32[16,130,1]{1,0,2:T(8,128)S(1)} %copy.150), channel_id=1, source_target_pairs={{1,0},{2,1},{3,2},{4,3},{5,4},{6,5},{7,6},{9,8},{10,9},{11,10},{12... | collective-permute-start | bytes 24968 | tf_op jit(solution)/shard_map/ppermute | solution.py:21
  112.2 5.6 %copy-start.21 = (f32[128,256,16]{1,2,0:T(8,128)S(1)}, f32[128,256,16]{1,2,0:T(8,128)}, u32[]{:S(2)}) copy-start(f32[128,256,16]{1,2,0:T(8,128)} %fusion.14) | copy-start | bytes 6291460
  112.2 5.6 %copy-start.22 = (f32[128,256,16]{1,2,0:T(8,128)S(1)}, f32[128,256,16]{1,2,0:T(8,128)}, u32[]{:S(2)}) copy-start(f32[128,256,16]{1,2,0:T(8,128)} %fusion.10) | copy-start | bytes 6291460
  115.0 2.8 copy-start.6
  115.0 2.8 copy-start.18
  122.0 9.9 %copy-start.7 = (f32[16,128,256]{2,0,1:T(8,128)}, f32[16,128,256]{2,0,1:T(8,128)S(1)}, u32[]{:S(2)}) copy-start(f32[16,128,256]{2,0,1:T(8,128)S(1)} %bitcast_add_fusion.1) | copy-start | bytes 6291460
  122.1 9.8 %collective-permute-start.8 = (f32[16,1,256]{2,0,1:T(8,128)S(1)}, f32[16,1,256]{2,0,1:T(8,128)S(1)}, u32[]{:S(2)}, u32[]{:S(2)}) collective-permute-start(f32[16,1,256]{2,0,1:T(8,128)S(1)} %get-tuple-element.15), channel_id=1, source_target_pairs={{0,8},{8,16},{16,24},{24,32},{32,40},{40,48},{48,56},{56,64},{64,7... | collective-permute-start | bytes 49160 | tf_op jit(solution)/shard_map/ppermute | solution.py:18
  126.0 5.9 %collective-permute-start.9 = (f32[16,1,256]{2,0,1:T(8,128)S(1)}, f32[16,1,256]{2,0,1:T(8,128)S(1)}, u32[]{:S(2)}, u32[]{:S(2)}) collective-permute-start(f32[16,1,256]{2,0,1:T(8,128)S(1)} %get-tuple-element.16), channel_id=1, source_target_pairs={{8,0},{16,8},{24,16},{32,24},{40,32},{48,40},{56,48},{64,56},{72,6... | collective-permute-start | bytes 49160 | tf_op jit(solution)/shard_map/ppermute | solution.py:21
  136.0 10.6 %copy-start.8 = (f32[16,128,256]{2,0,1:T(8,128)S(1)}, f32[16,128,256]{2,0,1:T(8,128)}, u32[]{:S(2)}) copy-start(f32[16,128,256]{2,0,1:T(8,128)} %copy-done.7) | copy-start | bytes 6291460
  136.0 15.3 %collective-permute-start.10 = (f32[16,130,1]{1,0,2:T(8,128)S(1)}, f32[16,130,1]{1,0,2:T(8,128)S(1)}, u32[]{:S(2)}, u32[]{:S(2)}) collective-permute-start(f32[16,130,1]{1,0,2:T(8,128)S(1)} %copy.152), channel_id=1, source_target_pairs={{0,1},{1,2},{2,3},{3,4},{4,5},{5,6},{6,7},{8,9},{9,10},{10,11},{11... | collective-permute-start | bytes 24968 | tf_op jit(solution)/shard_map/ppermute | solution.py:18
  140.4 10.1 %collective-permute-start.11 = (f32[16,130,1]{1,0,2:T(8,128)S(1)}, f32[16,130,1]{1,0,2:T(8,128)S(1)}, u32[]{:S(2)}, u32[]{:S(2)}) collective-permute-start(f32[16,130,1]{1,0,2:T(8,128)S(1)} %copy.154), channel_id=1, source_target_pairs={{1,0},{2,1},{3,2},{4,3},{5,4},{6,5},{7,6},{9,8},{10,9},{11,10},{12... | collective-permute-start | bytes 24968 | tf_op jit(solution)/shard_map/ppermute | solution.py:21
  164.7 5.6 %copy-start.19 = (f32[128,256,16]{1,2,0:T(8,128)S(1)}, f32[128,256,16]{1,2,0:T(8,128)}, u32[]{:S(2)}) copy-start(f32[128,256,16]{1,2,0:T(8,128)} %fusion.22) | copy-start | bytes 6291460
  164.7 5.6 %copy-start.20 = (f32[128,256,16]{1,2,0:T(8,128)S(1)}, f32[128,256,16]{1,2,0:T(8,128)}, u32[]{:S(2)}) copy-start(f32[128,256,16]{1,2,0:T(8,128)} %fusion.18) | copy-start | bytes 6291460
  167.5 2.8 copy-start.9
  167.6 2.8 copy-start.17
  211.6 2.3 copy-start.24
  211.6 19.2 %copy-start.26 = (bf16[2,256,256]{2,1,0:T(8,128)(2,1)S(1)}, bf16[2,256,256]{2,1,0:T(8,128)(2,1)}, u32[]{:S(2)}) copy-start(bf16[2,256,256]{2,1,0:T(8,128)(2,1)} %param.14) | copy-start | bytes 786436
  213.8 27.1 %copy-start.27 = (bf16[2,256,256]{2,1,0:T(8,128)(2,1)S(1)}, bf16[2,256,256]{2,1,0:T(8,128)(2,1)}, u32[]{:S(2)}) copy-start(bf16[2,256,256]{2,1,0:T(8,128)(2,1)} %param.15) | copy-start | bytes 786436
  215.1 22.4 %all-to-all-start = ((bf16[8,8,512]{2,1,0:T(8,128)(2,1)}), bf16[8,8,512]{2,1,0:T(8,128)(2,1)S(1)}, u32[]{:S(2)}, u32[]{:S(2)}) async-start(bf16[8,8,512]{2,1,0:T(8,128)(2,1)} %reshape_reshape.24), calls=%async_computation | async-start | bytes 131072 | tf_op jit(solution)/shard_map/all_to_all | solution.py:103
  237.5 10.4 %all-to-all-start.1 = ((bf16[8,8,512]{2,1,0:T(8,128)(2,1)}), bf16[8,8,512]{2,1,0:T(8,128)(2,1)S(1)}, u32[]{:S(2)}, u32[]{:S(2)}) async-start(bf16[8,8,512]{2,1,0:T(8,128)(2,1)} %reshape_reshape.25), calls=%async_computation.1 | async-start | bytes 131072 | tf_op jit(solution)/shard_map/all_to_all | solution.py:106
  247.9 10.2 %all-to-all-start.2 = ((bf16[8,8,512]{2,1,0:T(8,128)(2,1)}), bf16[8,8,512]{2,1,0:T(8,128)(2,1)S(1)}, u32[]{:S(2)}, u32[]{:S(2)}) async-start(bf16[8,8,512]{2,1,0:T(8,128)(2,1)} %reshape_reshape.26), calls=%async_computation.2 | async-start | bytes 131072 | tf_op jit(solution)/shard_map/all_to_all | solution.py:109
  301.7 6.2 %copy-start.25 = (bf16[2,256,256]{2,1,0:T(8,128)(2,1)S(1)}, bf16[2,256,256]{2,1,0:T(8,128)(2,1)}, u32[]{:S(2)}) copy-start(bf16[2,256,256]{2,1,0:T(8,128)(2,1)} %param.13) | copy-start | bytes 786436
  309.3 18.3 %all-to-all-start.4 = ((bf16[16,8,256]{2,1,0:T(8,128)(2,1)}), bf16[16,8,256]{2,1,0:T(8,128)(2,1)S(1)}, u32[]{:S(2)}, u32[]{:S(2)}) async-start(bf16[16,8,256]{2,1,0:T(8,128)(2,1)} %reshape_reshape.28), calls=%async_computation.4 | async-start | bytes 131072 | tf_op jit(solution)/shard_map/all_to_all | solution.py:123
  327.6 9.6 %all-to-all-start.5 = ((bf16[16,8,256]{2,1,0:T(8,128)(2,1)}), bf16[16,8,256]{2,1,0:T(8,128)(2,1)S(1)}, u32[]{:S(2)}, u32[]{:S(2)}) async-start(bf16[16,8,256]{2,1,0:T(8,128)(2,1)} %reshape_reshape.29), calls=%async_computation.5 | async-start | bytes 131072 | tf_op jit(solution)/shard_map/all_to_all | solution.py:126
  337.2 9.8 %all-to-all-start.6 = ((bf16[16,8,256]{2,1,0:T(8,128)(2,1)}), bf16[16,8,256]{2,1,0:T(8,128)(2,1)S(1)}, u32[]{:S(2)}, u32[]{:S(2)}) async-start(bf16[16,8,256]{2,1,0:T(8,128)(2,1)} %reshape_reshape.30), calls=%async_computation.6 | async-start | bytes 131072 | tf_op jit(solution)/shard_map/all_to_all | solution.py:129
  389.8 4.9 %copy-start.28 = (bf16[2,256,256]{2,1,0:T(8,128)(2,1)S(1)}, bf16[2,256,256]{2,1,0:T(8,128)(2,1)}, u32[]{:S(2)}) copy-start(bf16[2,256,256]{2,1,0:T(8,128)(2,1)} %param.16) | copy-start | bytes 786436
  (2 other events, 2.3 us)
where the time goes:
time: 451 us; the launch traced here: 443 us
  local copies, waits for them, and re-layouts  142 us (31%)
  matrix products  116 us (26%)
  starting transfers between devices  78.4 us (17%)
  other arithmetic  57.4 us (13%)
  waiting for transfers between devices  28.9 us (6%)
  blocking collectives  18.1 us (4%)
    dot_general x27, matrix products, advance(): jnp.einsum('dc,cxy->dxy', weights[index], padded[:, shift_r:shift_r + row...  106 us
    unnamed x2, other arithmetic  47 us
    reshape x2, local copies, waits for them, and re-layouts, unpatchify(): detail.reshape(leading, trailing, C, PATCH, PATCH).transpose(2, 0, 3, 1, 4)  28.1 us
    ppermute x6, starting transfers between devices, with_halo(): lax.ppermute(lax.slice_in_dim(block, block.shape[dim] - width, None, axis...  25.5 us
    reshape x2, local copies, waits for them, and re-layouts, patchify(): fine.reshape(channels, leading, PATCH, trailing, PATCH)  20.2 us
    unnamed x74, local copies, waits for them, and re-layouts  16.8 us
    all_to_all x1, starting transfers between devices, along_rows(): lax.all_to_all(queries.reshape(parts, -1, width), 'col', split_axis=0, co...  15.7 us
    reshape x1, local copies, waits for them, and re-layouts, patchify(): return fine.reshape(channels, leading, PATCH, trailing, PATCH).transpose(...  15.1 us
  transfers between devices with their start and end apart: 18, of which 6 were waited for; matrix products, arithmetic and copies ran while one was open for 15% of the time, Pallas kernels for 0%

commit v1 on v0

v1 whole, which is shorter than its diff:
```python
import jax
import jax.numpy as jnp
from jax import lax
from jax.experimental import pallas as pl
from jax.experimental.pallas import tpu as pltpu
from jax.sharding import PartitionSpec as P

C = 16
E = 256
H = 8
PATCH = 16
LAYERS = 3
NR = 16
NC = 8
TX = 128
TY = 256
CELLS = 128
U = TX + 16
W = TY + 128
G = 14
BF = jnp.bfloat16
F32 = jnp.float32
MESH = pl.DeviceIdType.MESH
NT = (((1,), (1,)), ((), ()))
TN = (((0,), (0,)), ((), ()))

STEPS = ((-1, 0), (1, 0), (0, -1), (0, 1), (-1, -1), (-1, 1), (1, -1), (1, 1))
OPPOSITE = (1, 0, 3, 2, 7, 6, 5, 4)


def iota2(shape, dim):
    return lax.broadcasted_iota(jnp.int32, shape, dim)


def ones_where(mask):
    return jnp.where(mask, 1.0, 0.0).astype(BF)


def swap_matrix():
    row = iota2((256, 256), 0)
    col = iota2((256, 256), 1)
    return ones_where(col == (row & 15) * 16 + (row >> 4))


def mm(a, b, dims=None):
    if dims is None:
        return jnp.dot(a, b, preferred_element_type=F32)
    return lax.dot_general(a, b, dims, preferred_element_type=F32)


def strip_select(k, size, near, far):
    row = iota2((32, size), 0)
    at = iota2((32, size), 1)
    s = (row & 15) - 4 * k
    goal = jnp.where(row < 16, near, far) + s
    return ones_where((s >= 0) & (s < 3) & (at == goal))


def strip_place(k):
    return strip_select(k, 128, 125, 0)


def normed(coarse):
    mean = jnp.mean(coarse * coarse, axis=-1, keepdims=True)
    return (coarse * lax.rsqrt(mean + 1e-06)).astype(BF)


def attend(cells, w_q, w_k, w_v):
    queries = mm(cells, w_q)
    lookups = mm(cells, w_k).astype(BF)
    values = mm(cells, w_v)
    head = iota2((128, E), 1) >> 5
    query_set = jnp.concatenate(
        [jnp.where(head == h, queries, 0.0).astype(BF) for h in range(H)], axis=0
    )
    scores = mm(query_set, lookups, NT) * (E // H) ** (-0.5)
    top = jnp.max(scores, axis=-1, keepdims=True)
    powers = jnp.exp(scores - top)
    weights = (powers / jnp.sum(powers, axis=-1, keepdims=True)).astype(BF)
    mixed = jnp.zeros((128, E), F32)
    for h in range(H):
        mixed = mixed + mm(
            weights[128 * h : 128 * (h + 1)], jnp.where(head == h, values, 0.0).astype(BF)
        )
    return mixed


def main_kernel(
    surface, coupling, w_stencil, w_patch, w_query, w_key, w_value, w_out,
    state_out, coarse_out,
    surf, cp, wst, wp, wq, wqkvo, sw, am, s_ref, bb, zt,
    row_s, col_s, row_r, col_r, corner_r,
    n0, g0, mix0, m0, n1, g1, mix1, m1,
    load_sem, store_sem, halo_send, halo_recv, a2a_send, a2a_recv,
):
    row = lax.axis_index("row")
    col = lax.axis_index("col")

    loads = []

    def load(src, dst):
        copy = pltpu.make_async_copy(src, dst, load_sem.at[len(loads)])
        copy.start()
        loads.append(copy)

    for i in range(8):
        load(surface.at[:, pl.ds(16 * i, 16), :], surf.at[:, pl.ds(16 * i, 16), :])
    for l in range(LAYERS):
        load(coupling.at[l], cp.at[l, pl.ds(8, TX), pl.ds(0, TY)])
    load(w_stencil, wst)
    load(w_patch, wp)
    for n, w in enumerate((w_query, w_key, w_value, w_out)):
        load(w, wqkvo.at[n])

    row_r[...] = jnp.zeros_like(row_r)
    col_r[...] = jnp.zeros_like(col_r)
    corner_r[...] = jnp.zeros_like(corner_r)

    def has(step):
        dr, dc = step
        ok = row >= 0
        if dr < 0:
            ok = row > 0
        if dr > 0:
            ok = row < NR - 1
        if dc < 0:
            ok = ok & (col > 0)
        if dc > 0:
            ok = ok & (col < NC - 1)
        return ok

    barrier = pltpu.get_barrier_semaphore()
    for d in range(1, NC):
        pl.semaphore_signal(
            barrier, inc=1, device_id=(row, lax.rem(col + d, NC)), device_id_type=MESH
        )
    for d in range(1, NR):
        pl.semaphore_signal(
            barrier, inc=1, device_id=(lax.rem(row + d, NR), col), device_id_type=MESH
        )
    expected = jnp.int32(NC - 1 + NR - 1)
    for step in STEPS[4:]:
        @pl.when(has(step))
        def _():
            pl.semaphore_signal(
                barrier, inc=1, device_id=(row + step[0], col + step[1]), device_id_type=MESH
            )

        expected = expected + jnp.where(has(step), 1, 0)

    sw[...] = swap_matrix()

    s_ref[0:80, 0:TY] = jnp.zeros((80, TY), F32)
    s_ref[139 * 16 : U * 16, 0:TY] = jnp.zeros((80, TY), F32)
    for buf in range(2):
        bb[buf, 0:32, :] = jnp.zeros((32, W), BF)
        bb[buf, 142 * 16 : U * 16, :] = jnp.zeros((32, W), BF)
    cp[2, 0:8, :] = jnp.zeros((8, W), F32)
    cp[2, 8 + TX : U, :] = jnp.zeros((8, W), F32)
    cp[2, 8 : 8 + TX, TY:W] = jnp.zeros((TX, 128), F32)

    loads[11].wait()
    spread = ones_where((iota2((C, 256), 1) & 15) == iota2((C, 256), 0))
    tiled = mm(wst[...].astype(BF), spread)
    band = iota2((C, 256), 1) >> 4
    for l in range(LAYERS):
        for b in range(3):
            pick = [
                tiled[((l * 9 + a * 3 + b) * C) : ((l * 9 + a * 3 + b) * C) + C] for a in range(3)
            ]
            for xo in range(G):
                block = jnp.where(
                    band == xo,
                    pick[0],
                    jnp.where(
                        band == xo + 1, pick[1], jnp.where(band == xo + 2, pick[2], 0.0)
                    ),
                )
                am[l, C * xo : C * (xo + 1), 256 * b : 256 * (b + 1)] = block.astype(BF)

    for i in range(8):
        loads[i].wait()
        block = surf[:, 16 * i : 16 * (i + 1), :].reshape(256, TY)
        high = block.astype(BF)
        low = (block - high.astype(F32)).astype(BF)
        turned = mm(sw[...], high)
        rows = pl.ds((8 + 16 * i) * C, 256)
        bb[0, rows, 0:TY] = turned.astype(BF)
        s_ref[rows, 0:TY] = turned + mm(sw[...], low)

    strip = jnp.zeros((32, 512), F32)
    for k in range(4):
        strip = strip + mm(
            strip_select(k, TY, 0, TY - 3), bb[0, pl.ds((8 + 32 * k) * C, 512), 0:TY], NT
        )
    strip = strip.astype(BF)
    for l in range(LAYERS):
        loads[8 + l].wait()
    cols = jnp.zeros((32, TX), F32)
    rows_c = jnp.zeros((32, TY), F32)
    for l in range(2):
        field = cp[l, 8 : 8 + TX, 0:TY].astype(BF)
        cols = cols + mm(strip_select(l, TY, 0, TY - 3), field, NT)
        rows_c = rows_c + mm(strip_select(l, TX, 0, TX - 3), field)
    cols = cols.astype(BF)
    rows_c = rows_c.astype(BF)
    for side in range(2):
        half = slice(16 * side, 16 * (side + 1))
        col_s[side, :, 0:128] = cols[half]
        col_s[side, :, 128:640] = strip[half]
        col_s[side, :, 640:768] = cols[half]
        row_s[side, 48:64, :] = rows_c[half]
    row_s[0, 0:48, :] = bb[0, 8 * C : 11 * C, 0:TY]
    row_s[1, 0:48, :] = bb[0, (5 + TX) * C : (8 + TX) * C, 0:TY]

    pl.semaphore_wait(barrier, expected)

    lower = pl.ds(0, 256)
    upper = pl.ds(512, 256)
    pieces = (
        (row_s.at[0], row_r.at[1]),
        (row_s.at[1], row_r.at[0]),
        (col_s.at[0], col_r.at[1]),
        (col_s.at[1], col_r.at[0]),
        (col_s.at[0, :, lower], corner_r.at[3]),
        (col_s.at[1, :, lower], corner_r.at[2]),
        (col_s.at[0, :, upper], corner_r.at[1]),
        (col_s.at[1, :, upper], corner_r.at[0]),
    )

    def halo_copy(d):
        src, dst = pieces[d]
        return pltpu.make_async_remote_copy(
            src_ref=src,
            dst_ref=dst,
            send_sem=halo_send.at[d],
            recv_sem=halo_recv.at[OPPOSITE[d]],
            device_id=(row + STEPS[d][0], col + STEPS[d][1]),
            device_id_type=MESH,
        )

    for d in range(8):
        @pl.when(has(STEPS[d]))
        def _():
            halo_copy(d).start()

    loads[12].wait()
    for p in range(PATCH):
        turned = mm(sw[...], wp[:, p, :, :].reshape(256, E))
        wq[:, C * p : C * (p + 1), :] = turned.astype(BF).reshape(PATCH, C, E)
    for n in range(4):
        loads[13 + n].wait()

    for d in range(8):
        @pl.when(has(STEPS[d]))
        def _():
            halo_copy(d).wait_send()

    for d in range(8):
        @pl.when(has(STEPS[d]))
        def _():
            halo_copy(OPPOSITE[d]).wait_recv()

    for side, u, first in ((0, 5, 5), (1, 8 + TX, 0)):
        s_ref[u * C : (u + 3) * C, 0:TY] = row_r[side, 0:48, :].astype(F32)
        for l in range(2):
            at = iota2((8, 16), 0) - first
            s = iota2((8, 16), 1) - 4 * l
            pick = ones_where((at == s) & (s >= 0) & (s < 3))
            top = 0 if side == 0 else 8 + TX
            cp[l, top : top + 8, 0:TY] = mm(pick, row_r[side, 48:64, :])
    both = jnp.concatenate([col_r[0, :, 128:640], col_r[1, :, 128:640]], axis=0)
    both_c = jnp.concatenate([col_r[0, :, 0:128], col_r[1, :, 0:128]], axis=0)
    for k in range(4):
        s_ref[pl.ds((8 + 32 * k) * C, 512), TY:W] = mm(both, strip_place(k), TN)
    for l in range(2):
        cp[l, 8 : 8 + TX, TY:W] = mm(both_c, strip_place(l), TN)
    above = jnp.concatenate([corner_r[0], corner_r[1]], axis=0)
    below = jnp.concatenate([corner_r[2], corner_r[3]], axis=0)
    s_ref[0 : 8 * C, TY:W] = mm(above[:, 0:128], strip_place(3), TN)
    s_ref[(8 + TX) * C : U * C, TY:W] = mm(below[:, 128:256], strip_place(0), TN)
    for l in range(2):
        cp[l, 0:8, TY:W] = mm(above[:, 128:256], strip_place(l), TN)[TX - 8 : TX]
        cp[l, 8 + TX : U, TY:W] = mm(below[:, 0:128], strip_place(l), TN)[0:8]

    for k in range(9):
        rows = pl.ds(256 * k, 256)
        bb[0, rows, :] = s_ref[rows, :].astype(BF)

    for l in range(LAYERS):
        src, dst = l % 2, (l + 1) % 2

        def group(k, carry):
            first = pl.multiple_of((1 + G * k) * C, C)
            window = bb[src, pl.ds(first, 256), :]
            stacked = jnp.concatenate(
                [
                    jnp.concatenate([window[:, W - 1 :], window[:, : W - 1]], axis=1),
                    window,
                    jnp.concatenate([window[:, 1:], window[:, :1]], axis=1),
                ],
                axis=0,
            )
            gain = jnp.tanh(mm(am[l], stacked))
            for x in range(G):
                rows = pl.ds(pl.multiple_of(first + C * (x + 1), C), C)
                factor = cp[l, pl.ds(2 + G * k + x, 1), :]
                new = s_ref[rows, :] + factor * gain[C * x : C * (x + 1)]
                s_ref[rows, :] = new
                bb[dst, rows, :] = new.astype(BF)
            return carry

        lax.fori_loop(0, 10, group, 0)

    last = LAYERS % 2
    for i in range(8):
        block = bb[last, pl.ds((8 + 16 * i) * C, 256), 0:TY]
        zt[i] = mm(sw[...], block, NT).astype(BF)
    coarse = jnp.zeros((CELLS, E), F32)
    for q in range(PATCH):
        coarse = coarse + mm(zt[:, 16 * q : 16 * (q + 1), :].reshape(CELLS, 256), wq[q])

    def a2a(phase, src, dst, peer_slot, peer, rows, me):
        return pltpu.make_async_remote_copy(
            src_ref=src.at[pl.ds(pl.multiple_of(peer_slot * rows, rows), rows)],
            dst_ref=dst.at[pl.ds(pl.multiple_of(me * rows, rows), rows)],
            send_sem=a2a_send.at[phase, peer_slot],
            recv_sem=a2a_recv.at[phase, me],
            device_id=peer,
            device_id_type=MESH,
        )

    def exchange(phase, src, dst, axis, between=None):
        size, rows, me = (NC, 16, col) if axis == "col" else (NR, 8, row)

        def peer_of(d):
            slot = lax.rem(me + d, size)
            return slot, ((row, slot) if axis == "col" else (slot, col))

        for d in range(1, size):
            slot, peer = peer_of(d)
            a2a(phase, src, dst, slot, peer, rows, me).start()
        own = pl.ds(pl.multiple_of(me * rows, rows), rows)
        dst[own, :] = src[own, :]
        if between is not None:
            between()
        for d in range(1, size):
            slot, peer = peer_of(d)
            a2a(phase, src, dst, slot, peer, rows, me).wait_send()
            a2a(phase, src, dst, me, peer, rows, slot).wait_recv()

    def state_back():
        for i in range(8):
            block = s_ref[pl.ds((8 + 16 * i) * C, 256), 0:TY]
            high = block.astype(BF)
            low = (block - high.astype(F32)).astype(BF)
            turned = mm(sw[...], high) + mm(sw[...], low)
            surf[:, 16 * i : 16 * (i + 1), :] = turned.reshape(C, 16, TY)
        pltpu.make_async_copy(surf, state_out, store_sem).start()

    n0[...] = normed(coarse)
    exchange(0, n0, g0, "col", state_back)
    mix0[...] = attend(g0[...], wqkvo[0, 0], wqkvo[1, 0], wqkvo[2, 0]).astype(BF)
    exchange(1, mix0, m0, "col")
    coarse = coarse + mm(m0[...], wqkvo[3, 0])

    r = iota2((CELLS, CELLS), 0)
    k = iota2((CELLS, CELLS), 1)
    turn = ones_where(k == (r & 7) * 16 + (r >> 3))
    n1[...] = mm(turn, normed(coarse))
    exchange(2, n1, g1, "row")
    mix1[...] = attend(g1[...].astype(BF), wqkvo[0, 1], wqkvo[1, 1], wqkvo[2, 1])
    exchange(3, mix1, m1, "row")
    back = mm(turn, m1[...].astype(BF), TN).astype(BF)
    coarse = coarse + mm(back, wqkvo[3, 1])
    coarse_out[...] = coarse.astype(BF)
    pltpu.make_async_copy(surf, state_out, store_sem).wait()


def unpatch_kernel(coarse, w_unpatch, state, out, sw, tt):
    @pl.when(pl.program_id(0) == 0)
    def _():
        sw[...] = swap_matrix()
        turned = []
        for c in range(C):
            turned.append(mm(sw[...], w_unpatch[:, 256 * c : 256 * (c + 1)], NT).astype(BF))
        for q in range(PATCH):
            weights = jnp.concatenate([t[16 * q : 16 * (q + 1)] for t in turned], axis=0)
            cells = mm(coarse[...], weights, NT).astype(BF)
            tt[:, 16 * q : 16 * (q + 1), :] = cells.reshape(8, 16, 256)

    detail = mm(tt[pl.program_id(0)], sw[...], TN)
    out[...] = state[...] + detail.reshape(C, 16, TY)


def on_device(surface, coupling, w_stencil, w_patch, w_query, w_key, w_value, w_out, w_unpatch):
    anywhere = pl.BlockSpec(memory_space=pl.ANY)
    state, coarse = pl.pallas_call(
        main_kernel,
        out_shape=(
            jax.ShapeDtypeStruct((C, TX, TY), F32),
            jax.ShapeDtypeStruct((CELLS, E), BF),
        ),
        in_specs=[anywhere] * 8,
        out_specs=(anywhere, pl.BlockSpec(memory_space=pltpu.VMEM)),
        scratch_shapes=[
            pltpu.VMEM((C, TX, TY), F32),
            pltpu.VMEM((LAYERS, U, W), F32),
            pltpu.VMEM((LAYERS * 9 * C, C), F32),
            pltpu.VMEM((C, PATCH, PATCH, E), BF),
            pltpu.VMEM((PATCH, 256, E), BF),
            pltpu.VMEM((4, 2, E, E), BF),
            pltpu.VMEM((256, 256), BF),
            pltpu.VMEM((LAYERS, G * C, 768), BF),
            pltpu.VMEM((U * C, W), F32),
            pltpu.VMEM((2, U * C, W), BF),
            pltpu.VMEM((8, 256, 256), BF),
            pltpu.VMEM((2, 64, TY), BF),
            pltpu.VMEM((2, 16, 768), BF),
            pltpu.VMEM((2, 64, TY), BF),
            pltpu.VMEM((2, 16, 768), BF),
            pltpu.VMEM((4, 16, 256), BF),
            pltpu.VMEM((CELLS, E), BF),
            pltpu.VMEM((CELLS, E), BF),
            pltpu.VMEM((CELLS, E), BF),
            pltpu.VMEM((CELLS, E), BF),
            pltpu.VMEM((CELLS, E), F32),
            pltpu.VMEM((CELLS, E), F32),
            pltpu.VMEM((CELLS, E), F32),
            pltpu.VMEM((CELLS, E), F32),
            pltpu.SemaphoreType.DMA((17,)),
            pltpu.SemaphoreType.DMA,
            pltpu.SemaphoreType.DMA((8,)),
            pltpu.SemaphoreType.DMA((8,)),
            pltpu.SemaphoreType.DMA((4, NR)),
            pltpu.SemaphoreType.DMA((4, NR)),
        ],
        compiler_params=pltpu.CompilerParams(
            collective_id=0, has_side_effects=True, vmem_limit_bytes=48 * 1024 * 1024
        ),
    )(
        surface,
        coupling,
        w_stencil.reshape(LAYERS * 9 * C, C),
        w_patch.reshape(C, PATCH, PATCH, E),
        w_query,
        w_key,
        w_value,
        w_out,
    )
    return pl.pallas_call(
        unpatch_kernel,
        grid=(8,),
        out_shape=jax.ShapeDtypeStruct((C, TX, TY), F32),
        in_specs=[
            pl.BlockSpec((CELLS, E), lambda i: (0, 0)),
            pl.BlockSpec((E, C * 256), lambda i: (0, 0)),
            pl.BlockSpec((C, 16, TY), lambda i: (0, i, 0)),
        ],
        out_specs=pl.BlockSpec((C, 16, TY), lambda i: (0, i, 0)),
        scratch_shapes=[pltpu.VMEM((256, 256), BF), pltpu.VMEM((8, 256, 256), BF)],
        compiler_params=pltpu.CompilerParams(vmem_limit_bytes=32 * 1024 * 1024),
    )(coarse, w_unpatch, state)


def solution(mesh):
    in_specs = (P(None, "row", "col"), P(None, "row", "col"), P(), P(), P(), P(), P(), P(), P())
    out_specs = P(None, "row", "col")
    return jax.shard_map(
        on_device, mesh=mesh, in_specs=in_specs, out_specs=out_specs, check_vma=False
    )
```

time: 451 us -> 63.5 us (0.14); the launches traced: 443 us -> 63.2 us
  local copies, waits for them, and re-layouts: 142 us -> 7.32 us
  matrix products: 116 us -> 0 us
  starting transfers between devices: 78.4 us -> 0 us
  other arithmetic: 57.4 us -> 0 us
  Pallas kernels: 0 us -> 55.9 us
  waiting for transfers between devices: 28.9 us -> 0 us
  blocking collectives: 18.1 us -> 0 us
    dot_general x40 -> x0, matrix products: 116 us -> none  [the longest x27 106 us: advance(): jnp.einsum('dc,cxy->dxy', weights[index], padded[:, shift_r:shift_r + row...]
    reshape x20 -> x0, local copies, waits for them, and re-layouts: 77.9 us -> none  [the longest x2 28.1 us: unpatchify(): detail.reshape(leading, trailing, C, PATCH, PATCH).transpose(2, 0, 3, 1, 4)]
    pallas_call x0 -> x2, Pallas kernels: none -> 55.9 us  [the longest x1 50.3 us: on_device(): pl.pallas_call(main_kernel, out_shape=(jax.ShapeDtypeStruct((C, TX, TY),...]
    unnamed x2 -> x0, other arithmetic: 47 us -> none
    all_to_all x6 -> x0, starting transfers between devices: 42.6 us -> none  [the longest x1 15.7 us: along_rows(): lax.all_to_all(queries.reshape(parts, -1, width), 'col', split_axis=0, co...]
    ppermute x12 -> x0, starting transfers between devices: 35.7 us -> none  [the longest x6 25.5 us: with_halo(): lax.ppermute(lax.slice_in_dim(block, block.shape[dim] - width, None, axis...]
    all_to_all x6 -> x0, waiting for transfers between devices: 28.8 us -> none  [the longest x1 5.73 us: along_rows(): lax.all_to_all(values.reshape(parts, -1, width), 'col', split_axis=0, con...]
    all_to_all x2 -> x0, blocking collectives: 18.1 us -> none  [the longest x1 9.11 us: along_rows(): lax.all_to_all(moved, 'col', split_axis=2, concat_axis=0, tiled=True)]
  transfers between devices with their start and end apart: 18 -> 0, of which waited for: 6 -> 0; matrix products, arithmetic and copies ran while one was open for 15% -> 0% of each run, Pallas kernels for 0% -> 0%
where the time goes in v1:
time: 63.5 us; the launch traced here: 63.2 us
  Pallas kernels  55.9 us (88%)
  local copies, waits for them, and re-layouts  7.32 us (12%)
    pallas_call x1, Pallas kernels, on_device(): pl.pallas_call(main_kernel, out_shape=(jax.ShapeDtypeStruct((C, TX, TY),...  50.3 us
    unnamed x16, local copies, waits for them, and re-layouts  7.32 us
    pallas_call x1, Pallas kernels, on_device(): pl.pallas_call(unpatch_kernel, grid=(8,), out_shape=jax.ShapeDtypeStruct(...  5.53 us

profile of v1, /device:TPU:1, one launch (start us, length us, event | category | flops | bytes accessed | tf_op | source)
XLA Modules:
  0.0 63.2 jit_solution(7665788954613093467)
XLA Ops:
  0.0 0.0 copy-start.1
  0.0 1.6 %copy-done.1 = f32[16,128,256]{2,1,0:T(8,128)S(1)} copy-done((f32[16,128,256]{2,1,0:T(8,128)S(1)}, f32[16,128,256]{2,1,0:T(8,128)}, u32[]{:S(2)}) %copy-start.1) | copy-done | bytes 2097176
  1.6 0.0 copy-start.2
  1.6 1.0 %copy-done.2 = f32[3,128,256]{2,1,0:T(8,128)S(1)} copy-done((f32[3,128,256]{2,1,0:T(8,128)S(1)}, f32[3,128,256]{2,1,0:T(8,128)}, u32[]{:S(2)}) %copy-start.2) | copy-done | bytes 393240
  2.6 0.0 copy-start.3
  2.6 0.9 %copy-done.3 = bf16[2,256,256]{2,1,0:T(8,128)(2,1)S(1)} copy-done((bf16[2,256,256]{2,1,0:T(8,128)(2,1)S(1)}, bf16[2,256,256]{2,1,0:T(8,128)(2,1)}, u32[]{:S(2)}) %copy-start.3) | copy-done | bytes 262168
  3.5 0.0 copy-start.4
  3.5 0.9 %copy-done.4 = bf16[2,256,256]{2,1,0:T(8,128)(2,1)S(1)} copy-done((bf16[2,256,256]{2,1,0:T(8,128)(2,1)S(1)}, bf16[2,256,256]{2,1,0:T(8,128)(2,1)}, u32[]{:S(2)}) %copy-start.4) | copy-done | bytes 262168
  4.5 0.0 copy-start.5
  4.5 0.9 %copy-done.5 = bf16[2,256,256]{2,1,0:T(8,128)(2,1)S(1)} copy-done((bf16[2,256,256]{2,1,0:T(8,128)(2,1)S(1)}, bf16[2,256,256]{2,1,0:T(8,128)(2,1)}, u32[]{:S(2)}) %copy-start.5) | copy-done | bytes 262168
  5.4 0.0 copy-start.6
  5.4 0.9 %copy-done.6 = bf16[2,256,256]{2,1,0:T(8,128)(2,1)S(1)} copy-done((bf16[2,256,256]{2,1,0:T(8,128)(2,1)S(1)}, bf16[2,256,256]{2,1,0:T(8,128)(2,1)}, u32[]{:S(2)}) %copy-start.6) | copy-done | bytes 262168
  6.4 0.0 copy-start.7
  6.4 0.9 %copy-done.7 = f32[3,9,16,16]{3,2,1,0:T(8,128)S(1)} copy-done((f32[3,9,16,16]{3,2,1,0:T(8,128)S(1)}, f32[3,9,16,16]{3,2,1,0:T(8,128)}, u32[]{:S(2)}) %copy-start.7) | copy-done | bytes 27672
  7.3 0.0 copy-start
  7.3 50.3 %shard_map.91 = (f32[16,128,256]{2,1,0:T(8,128)S(1)}, bf16[128,256]{1,0:T(8,128)(2,1)S(1)}) custom-call(f32[16,128,256]{2,1,0:T(8,128)S(1)} %copy-done.1, f32[3,128,256]{2,1,0:T(8,128)S(1)} %copy-done.2, f32[432,16]{1,0:T(8,128)S(1)} %bitcast.2, bf16[16,16,16,256]{3,2,1,0:T(8,128)(2,1)} %bitcast.3, bf16[2,256,256]{2,1,0:T(8,128)(2,1)S(1)} %copy-done.3, ...), custom_call_target="tpu_custom_call" | custom-call | tf_op jit(solution)/shard_map/pallas_call | solution.py:398
  57.7 0.0 copy-done
  57.7 5.5 %shard_map.92 = f32[16,128,256]{2,1,0:T(8,128)} custom-call(bf16[128,256]{1,0:T(8,128)(2,1)S(1)} %get-tuple-element.7.coarse, bf16[256,4096]{1,0:T(8,128)(2,1)S(1)} %copy-done, f32[16,128,256]{2,1,0:T(8,128)S(1)} %get-tuple-element.8.state), custom_call_target="tpu_custom_call" | custom-call | tf_op jit(solution)/shard_map/pallas_call | solution.py:451
Async XLA Ops:
  0.0 1.6 %copy-start.1 = (f32[16,128,256]{2,1,0:T(8,128)S(1)}, f32[16,128,256]{2,1,0:T(8,128)}, u32[]{:S(2)}) copy-start(f32[16,128,256]{2,1,0:T(8,128)} %surface.1) | copy-start | bytes 6291460
  1.6 1.0 %copy-start.2 = (f32[3,128,256]{2,1,0:T(8,128)S(1)}, f32[3,128,256]{2,1,0:T(8,128)}, u32[]{:S(2)}) copy-start(f32[3,128,256]{2,1,0:T(8,128)} %coupling.1) | copy-start | bytes 1179652
  2.6 0.9 %copy-start.3 = (bf16[2,256,256]{2,1,0:T(8,128)(2,1)S(1)}, bf16[2,256,256]{2,1,0:T(8,128)(2,1)}, u32[]{:S(2)}) copy-start(bf16[2,256,256]{2,1,0:T(8,128)(2,1)} %w_query.1) | copy-start | bytes 786436
  3.5 0.9 %copy-start.4 = (bf16[2,256,256]{2,1,0:T(8,128)(2,1)S(1)}, bf16[2,256,256]{2,1,0:T(8,128)(2,1)}, u32[]{:S(2)}) copy-start(bf16[2,256,256]{2,1,0:T(8,128)(2,1)} %w_key.1) | copy-start | bytes 786436
  4.5 0.9 %copy-start.5 = (bf16[2,256,256]{2,1,0:T(8,128)(2,1)S(1)}, bf16[2,256,256]{2,1,0:T(8,128)(2,1)}, u32[]{:S(2)}) copy-start(bf16[2,256,256]{2,1,0:T(8,128)(2,1)} %w_value.1) | copy-start | bytes 786436
  5.4 0.9 %copy-start.6 = (bf16[2,256,256]{2,1,0:T(8,128)(2,1)S(1)}, bf16[2,256,256]{2,1,0:T(8,128)(2,1)}, u32[]{:S(2)}) copy-start(bf16[2,256,256]{2,1,0:T(8,128)(2,1)} %w_out.1) | copy-start | bytes 786436
  6.4 0.9 %copy-start.7 = (f32[3,9,16,16]{3,2,1,0:T(8,128)S(1)}, f32[3,9,16,16]{3,2,1,0:T(8,128)}, u32[]{:S(2)}) copy-start(f32[3,9,16,16]{3,2,1,0:T(8,128)} %param.11) | copy-start | bytes 82948
  7.3 50.3 %copy-start = (bf16[256,4096]{1,0:T(8,128)(2,1)S(1)}, bf16[256,4096]{1,0:T(8,128)(2,1)}, u32[]{:S(2)}) copy-start(bf16[256,4096]{1,0:T(8,128)(2,1)} %w_unpatch.1) | copy-start | bytes 6291460

commit v2 on v1

--- a/solution.py
+++ b/solution.py
@@ -86,9 +86,9 @@
 
 
 def main_kernel(
-    surface, coupling, w_stencil, w_patch, w_query, w_key, w_value, w_out,
-    state_out, coarse_out,
-    surf, cp, wst, wp, wq, wqkvo, sw, am, s_ref, bb, zt,
+    surface, coupling, w_stencil, w_patch, w_query, w_key, w_value, w_out, w_unpatch,
+    out,
+    surf, cp, wst, wp, wu, wq, wqkvo, sw, am, s_ref, bb, zt,
     row_s, col_s, row_r, col_r, corner_r,
     n0, g0, mix0, m0, n1, g1, mix1, m1,
     load_sem, store_sem, halo_send, halo_recv, a2a_send, a2a_recv,
@@ -111,6 +111,7 @@
     load(w_patch, wp)
     for n, w in enumerate((w_query, w_key, w_value, w_out)):
         load(w, wqkvo.at[n])
+    load(w_unpatch, wu)
 
     row_r[...] = jnp.zeros_like(row_r)
     col_r[...] = jnp.zeros_like(col_r)
@@ -149,34 +150,6 @@
         expected = expected + jnp.where(has(step), 1, 0)
 
     sw[...] = swap_matrix()
-
-    s_ref[0:80, 0:TY] = jnp.zeros((80, TY), F32)
-    s_ref[139 * 16 : U * 16, 0:TY] = jnp.zeros((80, TY), F32)
-    for buf in range(2):
-        bb[buf, 0:32, :] = jnp.zeros((32, W), BF)
-        bb[buf, 142 * 16 : U * 16, :] = jnp.zeros((32, W), BF)
-    cp[2, 0:8, :] = jnp.zeros((8, W), F32)
-    cp[2, 8 + TX : U, :] = jnp.zeros((8, W), F32)
-    cp[2, 8 : 8 + TX, TY:W] = jnp.zeros((TX, 128), F32)
-
-    loads[11].wait()
-    spread = ones_where((iota2((C, 256), 1) & 15) == iota2((C, 256), 0))
-    tiled = mm(wst[...].astype(BF), spread)
-    band = iota2((C, 256), 1) >> 4
-    for l in range(LAYERS):
-        for b in range(3):
-            pick = [
-                tiled[((l * 9 + a * 3 + b) * C) : ((l * 9 + a * 3 + b) * C) + C] for a in range(3)
-            ]
-            for xo in range(G):
-                block = jnp.where(
-                    band == xo,
-                    pick[0],
-                    jnp.where(
-                        band == xo + 1, pick[1], jnp.where(band == xo + 2, pick[2], 0.0)
-                    ),
-                )
-                am[l, C * xo : C * (xo + 1), 256 * b : 256 * (b + 1)] = block.astype(BF)
 
     for i in range(8):
         loads[i].wait()
@@ -244,6 +217,35 @@
         def _():
             halo_copy(d).start()
 
+    s_ref[0:80, 0:TY] = jnp.zeros((80, TY), F32)
+    s_ref[139 * 16 : U * 16, 0:TY] = jnp.zeros((80, TY), F32)
+    bb[0, 0:80, 0:TY] = jnp.zeros((80, TY), BF)
+    bb[0, 139 * 16 : U * 16, 0:TY] = jnp.zeros((80, TY), BF)
+    bb[1, 0:96, :] = jnp.zeros((96, W), BF)
+    bb[1, 138 * 16 : U * 16, :] = jnp.zeros((96, W), BF)
+    cp[2, 0:8, :] = jnp.zeros((8, W), F32)
+    cp[2, 8 + TX : U, :] = jnp.zeros((8, W), F32)
+    cp[2, 8 : 8 + TX, TY:W] = jnp.zeros((TX, 128), F32)
+
+    loads[11].wait()
+    spread = ones_where((iota2((C, 256), 1) & 15) == iota2((C, 256), 0))
+    tiled = mm(wst[...].astype(BF), spread)
+    band = iota2((C, 256), 1) >> 4
+    for l in range(LAYERS):
+        for b in range(3):
+            pick = [
+                tiled[((l * 9 + a * 3 + b) * C) : ((l * 9 + a * 3 + b) * C) + C] for a in range(3)
+            ]
+            for xo in range(G):
+                block = jnp.where(
+                    band == xo,
+                    pick[0],
+                    jnp.where(
+                        band == xo + 1, pick[1], jnp.where(band == xo + 2, pick[2], 0.0)
+                    ),
+                )
+                am[l, C * xo : C * (xo + 1), 256 * b : 256 * (b + 1)] = block.astype(BF)
+
     loads[12].wait()
     for p in range(PATCH):
         turned = mm(sw[...], wp[:, p, :, :].reshape(256, E))
@@ -254,63 +256,67 @@
     for d in range(8):
         @pl.when(has(STEPS[d]))
         def _():
-            halo_copy(d).wait_send()
-
-    for d in range(8):
-        @pl.when(has(STEPS[d]))
-        def _():
             halo_copy(OPPOSITE[d]).wait_recv()
 
     for side, u, first in ((0, 5, 5), (1, 8 + TX, 0)):
-        s_ref[u * C : (u + 3) * C, 0:TY] = row_r[side, 0:48, :].astype(F32)
+        halo = row_r[side, 0:48, :]
+        s_ref[u * C : (u + 3) * C, 0:TY] = halo.astype(F32)
+        bb[0, u * C : (u + 3) * C, 0:TY] = halo
         for l in range(2):
             at = iota2((8, 16), 0) - first
             s = iota2((8, 16), 1) - 4 * l
             pick = ones_where((at == s) & (s >= 0) & (s < 3))
             top = 0 if side == 0 else 8 + TX
             cp[l, top : top + 8, 0:TY] = mm(pick, row_r[side, 48:64, :])
+    def place(rows, strip, k):
+        columns = mm(strip, strip_place(k), TN)
+        s_ref[rows, TY:W] = columns
+        bb[0, rows, TY:W] = columns.astype(BF)
+
     both = jnp.concatenate([col_r[0, :, 128:640], col_r[1, :, 128:640]], axis=0)
     both_c = jnp.concatenate([col_r[0, :, 0:128], col_r[1, :, 0:128]], axis=0)
     for k in range(4):
-        s_ref[pl.ds((8 + 32 * k) * C, 512), TY:W] = mm(both, strip_place(k), TN)
+        place(pl.ds((8 + 32 * k) * C, 512), both, k)
     for l in range(2):
         cp[l, 8 : 8 + TX, TY:W] = mm(both_c, strip_place(l), TN)
     above = jnp.concatenate([corner_r[0], corner_r[1]], axis=0)
     below = jnp.concatenate([corner_r[2], corner_r[3]], axis=0)
-    s_ref[0 : 8 * C, TY:W] = mm(above[:, 0:128], strip_place(3), TN)
-    s_ref[(8 + TX) * C : U * C, TY:W] = mm(below[:, 128:256], strip_place(0), TN)
+    place(pl.ds(0, 128), above[:, 0:128], 3)
+    place(pl.ds((8 + TX) * C, 128), below[:, 128:256], 0)
     for l in range(2):
         cp[l, 0:8, TY:W] = mm(above[:, 128:256], strip_place(l), TN)[TX - 8 : TX]
         cp[l, 8 + TX : U, TY:W] = mm(below[:, 0:128], strip_place(l), TN)[0:8]
 
-    for k in range(9):
-        rows = pl.ds(256 * k, 256)
-        bb[0, rows, :] = s_ref[rows, :].astype(BF)
-
     for l in range(LAYERS):
         src, dst = l % 2, (l + 1) % 2
-
-        def group(k, carry):
-            first = pl.multiple_of((1 + G * k) * C, C)
-            window = bb[src, pl.ds(first, 256), :]
-            stacked = jnp.concatenate(
-                [
-                    jnp.concatenate([window[:, W - 1 :], window[:, : W - 1]], axis=1),
-                    window,
-                    jnp.concatenate([window[:, 1:], window[:, :1]], axis=1),
-                ],
-                axis=0,
+        wide = W if l < LAYERS - 1 else TY
+        for k in range(10):
+            u = 6 + l + G * k
+            count = G if k < 9 else 6
+            depth = (count + 2) * C
+            window = bb[src, (u - 1) * C : (u - 1) * C + depth, :]
+            shifted = (
+                jnp.concatenate([window[:, W - 1 :], window[:, : wide - 1]], axis=1),
+                window[:, :wide],
+                jnp.concatenate([window[:, 1:], window[:, :1]], axis=1)[:, :wide],
             )
-            gain = jnp.tanh(mm(am[l], stacked))
-            for x in range(G):
-                rows = pl.ds(pl.multiple_of(first + C * (x + 1), C), C)
-                factor = cp[l, pl.ds(2 + G * k + x, 1), :]
-                new = s_ref[rows, :] + factor * gain[C * x : C * (x + 1)]
-                s_ref[rows, :] = new
-                bb[dst, rows, :] = new.astype(BF)
-            return carry
-
-        lax.fori_loop(0, 10, group, 0)
+            if count == G:
+                mix = mm(am[l], jnp.concatenate(shifted, axis=0))
+            else:
+                mix = sum(
+                    mm(am[l, 0 : count * C, 256 * b : 256 * b + depth], shifted[b])
+                    for b in range(3)
+                )
+            gain = jnp.tanh(mix)
+            for x in range(count):
+                if u + x > 137 - l:
+                    continue
+                rows = slice((u + x) * C, (u + x + 1) * C)
+                new = s_ref[rows, :wide] + cp[l, u + x : u + x + 1, :wide] * (
+                    gain[C * x : C * (x + 1)]
+                )
+                s_ref[rows, :wide] = new
+                bb[dst, rows, :wide] = new.astype(BF)
 
     last = LAYERS % 2
     for i in range(8):
@@ -346,8 +352,14 @@
             between()
         for d in range(1, size):
             slot, peer = peer_of(d)
-            a2a(phase, src, dst, slot, peer, rows, me).wait_send()
             a2a(phase, src, dst, me, peer, rows, slot).wait_recv()
+
+        def sent():
+            for d in range(1, size):
+                slot, peer = peer_of(d)
+                a2a(phase, src, dst, slot, peer, rows, me).wait_send()
+
+        return sent
 
     def state_back():
         for i in range(8):
@@ -356,58 +368,64 @@
             low = (block - high.astype(F32)).astype(BF)
             turned = mm(sw[...], high) + mm(sw[...], low)
             surf[:, 16 * i : 16 * (i + 1), :] = turned.reshape(C, 16, TY)
-        pltpu.make_async_copy(surf, state_out, store_sem).start()
+
+    def unpatch_weights():
+        loads[17].wait()
+        for c in range(C):
+            turned = mm(sw[...], wu[:, 256 * c : 256 * (c + 1)], NT).astype(BF)
+            wq[:, C * c : C * (c + 1), :] = turned.reshape(PATCH, C, E)
 
     n0[...] = normed(coarse)
-    exchange(0, n0, g0, "col", state_back)
+    sent0 = exchange(0, n0, g0, "col", state_back)
     mix0[...] = attend(g0[...], wqkvo[0, 0], wqkvo[1, 0], wqkvo[2, 0]).astype(BF)
-    exchange(1, mix0, m0, "col")
+    sent1 = exchange(1, mix0, m0, "col", unpatch_weights)
     coarse = coarse + mm(m0[...], wqkvo[3, 0])
 
     r = iota2((CELLS, CELLS), 0)
     k = iota2((CELLS, CELLS), 1)
     turn = ones_where(k == (r & 7) * 16 + (r >> 3))
     n1[...] = mm(turn, normed(coarse))
-    exchange(2, n1, g1, "row")
+    sent2 = exchange(2, n1, g1, "row")
     mix1[...] = attend(g1[...].astype(BF), wqkvo[0, 1], wqkvo[1, 1], wqkvo[2, 1])
-    exchange(3, mix1, m1, "row")
+    sent3 = exchange(3, mix1, m1, "row")
     back = mm(turn, m1[...].astype(BF), TN).astype(BF)
     coarse = coarse + mm(back, wqkvo[3, 1])
-    coarse_out[...] = coarse.astype(BF)
-    pltpu.make_async_copy(surf, state_out, store_sem).wait()
-
-
-def unpatch_kernel(coarse, w_unpatch, state, out, sw, tt):
-    @pl.when(pl.program_id(0) == 0)
-    def _():
-        sw[...] = swap_matrix()
-        turned = []
-        for c in range(C):
-            turned.append(mm(sw[...], w_unpatch[:, 256 * c : 256 * (c + 1)], NT).astype(BF))
-        for q in range(PATCH):
-            weights = jnp.concatenate([t[16 * q : 16 * (q + 1)] for t in turned], axis=0)
-            cells = mm(coarse[...], weights, NT).astype(BF)
-            tt[:, 16 * q : 16 * (q + 1), :] = cells.reshape(8, 16, 256)
-
-    detail = mm(tt[pl.program_id(0)], sw[...], TN)
-    out[...] = state[...] + detail.reshape(C, 16, TY)
+    coarse = coarse.astype(BF)
+    for q in range(PATCH):
+        cells = mm(coarse, wq[q], NT).astype(BF)
+        zt[:, 16 * q : 16 * (q + 1), :] = cells.reshape(8, 16, 256)
+    stores = []
+    for i in range(8):
+        rows = slice(16 * i, 16 * (i + 1))
+        detail = mm(zt[i], sw[...], TN)
+        surf[:, rows, :] = surf[:, rows, :] + detail.reshape(C, 16, TY)
+        copy = pltpu.make_async_copy(surf.at[:, rows, :], out.at[:, rows, :], store_sem.at[i])
+        copy.start()
+        stores.append(copy)
+    for d in range(8):
+        @pl.when(has(STEPS[d]))
+        def _():
+            halo_copy(d).wait_send()
+
+    for sent in (sent0, sent1, sent2, sent3):
+        sent()
+    for copy in stores:
+        copy.wait()
 
 
 def on_device(surface, coupling, w_stencil, w_patch, w_query, w_key, w_value, w_out, w_unpatch):
     anywhere = pl.BlockSpec(memory_space=pl.ANY)
-    state, coarse = pl.pallas_call(
+    return pl.pallas_call(
         main_kernel,
-        out_shape=(
-            jax.ShapeDtypeStruct((C, TX, TY), F32),
-            jax.ShapeDtypeStruct((CELLS, E), BF),
-        ),
-        in_specs=[anywhere] * 8,
-        out_specs=(anywhere, pl.BlockSpec(memory_space=pltpu.VMEM)),
+        out_shape=jax.ShapeDtypeStruct((C, TX, TY), F32),
+        in_specs=[anywhere] * 9,
+        out_specs=anywhere,
         scratch_shapes=[
             pltpu.VMEM((C, TX, TY), F32),
             pltpu.VMEM((LAYERS, U, W), F32),
             pltpu.VMEM((LAYERS * 9 * C, C), F32),
             pltpu.VMEM((C, PATCH, PATCH, E), BF),
+            pltpu.VMEM((E, C * 256), BF),
             pltpu.VMEM((PATCH, 256, E), BF),
             pltpu.VMEM((4, 2, E, E), BF),
             pltpu.VMEM((256, 256), BF),
@@ -428,15 +446,15 @@
             pltpu.VMEM((CELLS, E), F32),
             pltpu.VMEM((CELLS, E), F32),
             pltpu.VMEM((CELLS, E), F32),
-            pltpu.SemaphoreType.DMA((17,)),
-            pltpu.SemaphoreType.DMA,
+            pltpu.SemaphoreType.DMA((18,)),
+            pltpu.SemaphoreType.DMA((8,)),
             pltpu.SemaphoreType.DMA((8,)),
             pltpu.SemaphoreType.DMA((8,)),
             pltpu.SemaphoreType.DMA((4, NR)),
             pltpu.SemaphoreType.DMA((4, NR)),
         ],
         compiler_params=pltpu.CompilerParams(
-            collective_id=0, has_side_effects=True, vmem_limit_bytes=48 * 1024 * 1024
+            collective_id=0, has_side_effects=True, vmem_limit_bytes=60 * 1024 * 1024
         ),
     )(
         surface,
@@ -447,20 +465,8 @@
         w_key,
         w_value,
         w_out,
+        w_unpatch,
     )
-    return pl.pallas_call(
-        unpatch_kernel,
-        grid=(8,),
-        out_shape=jax.ShapeDtypeStruct((C, TX, TY), F32),
-        in_specs=[
-            pl.BlockSpec((CELLS, E), lambda i: (0, 0)),
-            pl.BlockSpec((E, C * 256), lambda i: (0, 0)),
-            pl.BlockSpec((C, 16, TY), lambda i: (0, i, 0)),
-        ],
-        out_specs=pl.BlockSpec((C, 16, TY), lambda i: (0, i, 0)),
-        scratch_shapes=[pltpu.VMEM((256, 256), BF), pltpu.VMEM((8, 256, 256), BF)],
-        compiler_params=pltpu.CompilerParams(vmem_limit_bytes=32 * 1024 * 1024),
-    )(coarse, w_unpatch, state)
 
 
 def solution(mesh):

time: 63.5 us -> 45.9 us (0.72)
  Pallas kernels: 55.9 us -> 42.6 us
  local copies, waits for them, and re-layouts: 7.32 us -> 3.1 us
    pallas_call x2 -> x1, Pallas kernels: 55.9 us -> 42.6 us  [on_device(): pl.pallas_call(main_kernel, out_shape=jax.ShapeDtypeStruct((C, TX, TY), F...]
    unnamed x16 -> x1, local copies, waits for them, and re-layouts: 7.32 us -> 3.1 us
where the time goes in v2:
time: 45.9 us; the launch traced here: 45.8 us
  Pallas kernels  42.6 us (93%)
  local copies, waits for them, and re-layouts  3.1 us (7%)
    pallas_call x1, Pallas kernels, on_device(): pl.pallas_call(main_kernel, out_shape=jax.ShapeDtypeStruct((C, TX, TY), F...  42.6 us
    unnamed x1, local copies, waits for them, and re-layouts  3.1 us

profile of v2, /device:TPU:1, one launch (start us, length us, event | category | flops | bytes accessed | tf_op | source)
XLA Modules:
  0.0 45.8 jit_solution(1053563548800625777)
XLA Ops:
  0.0 42.6 %shard_map.91 = f32[16,128,256]{2,1,0:T(8,128)} custom-call(f32[16,128,256]{2,1,0:T(8,128)} %surface.1, f32[3,128,256]{2,1,0:T(8,128)} %coupling.1, f32[432,16]{1,0:T(8,128)} %bitcast.3, bf16[16,16,16,256]{3,2,1,0:T(8,128)(2,1)} %bitcast.2, bf16[2,256,256]{2,1,0:T(8,128)(2,1)} %w_query.1, bf16[2,256,256]{2,1,0:T(8,128)(2,1)} %w_key.1, ...), custom_call_target="tpu_custom_call" | custom-call | tf_op jit(solution)/shard_map/pallas_call | solution.py:418
  42.7 3.1 %copy.11 = f32[16,128,256]{2,1,0:T(8,128)} copy(f32[16,128,256]{2,1,0:T(8,128)} %shard_map.91) | data formatting | bytes 4194304

commit v3 on v2

--- a/solution.py
+++ b/solution.py
@@ -87,11 +87,11 @@
 
 def main_kernel(
     surface, coupling, w_stencil, w_patch, w_query, w_key, w_value, w_out, w_unpatch,
-    out,
-    surf, cp, wst, wp, wu, wq, wqkvo, sw, am, s_ref, bb, zt,
+    state, zt,
+    surf, cp, wst, wp, wu, wq, wqkvo, sw, am, s_ref, bb,
     row_s, col_s, row_r, col_r, corner_r,
     n0, g0, mix0, m0, n1, g1, mix1, m1,
-    load_sem, store_sem, halo_send, halo_recv, a2a_send, a2a_recv,
+    load_sem, halo_send, halo_recv, a2a_send, a2a_recv,
 ):
     row = lax.axis_index("row")
     col = lax.axis_index("col")
@@ -367,7 +367,7 @@
             high = block.astype(BF)
             low = (block - high.astype(F32)).astype(BF)
             turned = mm(sw[...], high) + mm(sw[...], low)
-            surf[:, 16 * i : 16 * (i + 1), :] = turned.reshape(C, 16, TY)
+            state[:, 16 * i : 16 * (i + 1), :] = turned.reshape(C, 16, TY)
 
     def unpatch_weights():
         loads[17].wait()
@@ -394,14 +394,6 @@
     for q in range(PATCH):
         cells = mm(coarse, wq[q], NT).astype(BF)
         zt[:, 16 * q : 16 * (q + 1), :] = cells.reshape(8, 16, 256)
-    stores = []
-    for i in range(8):
-        rows = slice(16 * i, 16 * (i + 1))
-        detail = mm(zt[i], sw[...], TN)
-        surf[:, rows, :] = surf[:, rows, :] + detail.reshape(C, 16, TY)
-        copy = pltpu.make_async_copy(surf.at[:, rows, :], out.at[:, rows, :], store_sem.at[i])
-        copy.start()
-        stores.append(copy)
     for d in range(8):
         @pl.when(has(STEPS[d]))
         def _():
@@ -409,17 +401,30 @@
 
     for sent in (sent0, sent1, sent2, sent3):
         sent()
+
+
+def add_kernel(zt, state, out, swap, held, store_sem):
+    swap[...] = swap_matrix()
+    stores = []
+    for i in range(8):
+        rows = slice(16 * i, 16 * (i + 1))
+        detail = mm(zt[i], swap[...], TN)
+        held[:, rows, :] = state[:, rows, :] + detail.reshape(C, 16, TY)
+        copy = pltpu.make_async_copy(held.at[:, rows, :], out.at[:, rows, :], store_sem.at[i])
+        copy.start()
+        stores.append(copy)
     for copy in stores:
         copy.wait()
 
 
 def on_device(surface, coupling, w_stencil, w_patch, w_query, w_key, w_value, w_out, w_unpatch):
     anywhere = pl.BlockSpec(memory_space=pl.ANY)
-    return pl.pallas_call(
+    in_vmem = pl.BlockSpec(memory_space=pltpu.VMEM)
+    state, cells = pl.pallas_call(
         main_kernel,
-        out_shape=jax.ShapeDtypeStruct((C, TX, TY), F32),
+        out_shape=(pltpu.VMEM((C, TX, TY), F32), pltpu.VMEM((8, 256, 256), BF)),
         in_specs=[anywhere] * 9,
-        out_specs=anywhere,
+        out_specs=(in_vmem, in_vmem),
         scratch_shapes=[
             pltpu.VMEM((C, TX, TY), F32),
             pltpu.VMEM((LAYERS, U, W), F32),
@@ -432,7 +437,6 @@
             pltpu.VMEM((LAYERS, G * C, 768), BF),
             pltpu.VMEM((U * C, W), F32),
             pltpu.VMEM((2, U * C, W), BF),
-            pltpu.VMEM((8, 256, 256), BF),
             pltpu.VMEM((2, 64, TY), BF),
             pltpu.VMEM((2, 16, 768), BF),
             pltpu.VMEM((2, 64, TY), BF),
@@ -447,7 +451,6 @@
             pltpu.VMEM((CELLS, E), F32),
             pltpu.VMEM((CELLS, E), F32),
             pltpu.SemaphoreType.DMA((18,)),
-            pltpu.SemaphoreType.DMA((8,)),
             pltpu.SemaphoreType.DMA((8,)),
             pltpu.SemaphoreType.DMA((8,)),
             pltpu.SemaphoreType.DMA((4, NR)),
@@ -467,6 +470,18 @@
         w_out,
         w_unpatch,
     )
+    return pl.pallas_call(
+        add_kernel,
+        out_shape=jax.ShapeDtypeStruct((C, TX, TY), F32),
+        in_specs=[in_vmem, in_vmem],
+        out_specs=anywhere,
+        scratch_shapes=[
+            pltpu.VMEM((256, 256), BF),
+            pltpu.VMEM((C, TX, TY), F32),
+            pltpu.SemaphoreType.DMA((8,)),
+        ],
+        compiler_params=pltpu.CompilerParams(vmem_limit_bytes=32 * 1024 * 1024),
+    )(cells, state)
 
 
 def solution(mesh):

time: 45.9 us -> 42.8 us (0.932)
  local copies, waits for them, and re-layouts: 3.1 us -> 0 us
    unnamed x1 -> x0, local copies, waits for them, and re-layouts: 3.1 us -> none
    pallas_call x1 -> x2, Pallas kernels: 42.6 us -> 42.7 us  [the longest x1 41 us: on_device(): pl.pallas_call(main_kernel, out_shape=(pltpu.VMEM((C, TX, TY), F32), pltp...]
where the time goes in v3:
time: 42.8 us; the launch traced here: 42.7 us
  Pallas kernels  42.7 us (100%)
    pallas_call x1, Pallas kernels, on_device(): pl.pallas_call(main_kernel, out_shape=(pltpu.VMEM((C, TX, TY), F32), pltp...  41 us
    pallas_call x1, Pallas kernels, on_device(): pl.pallas_call(add_kernel, out_shape=jax.ShapeDtypeStruct((C, TX, TY), F3...  1.63 us

profile of v3, /device:TPU:1, one launch (start us, length us, event | category | flops | bytes accessed | tf_op | source)
XLA Modules:
  0.0 42.7 jit_solution(4446913027236261893)
XLA Ops:
  0.0 41.0 %shard_map.91 = (f32[16,128,256]{2,1,0:T(8,128)S(1)}, bf16[8,256,256]{2,1,0:T(8,128)(2,1)S(1)}) custom-call(f32[16,128,256]{2,1,0:T(8,128)} %surface.1, f32[3,128,256]{2,1,0:T(8,128)} %coupling.1, f32[432,16]{1,0:T(8,128)} %bitcast.3, bf16[16,16,16,256]{3,2,1,0:T(8,128)(2,1)} %bitcast.2, bf16[2,256,256]{2,1,0:T(8,128)(2,1)} %w_query.1, ...), custom_call_target="tpu_custom_call" | custom-call | tf_op jit(solution)/shard_map/pallas_call | solution.py:423
  41.0 1.6 %shard_map.92 = f32[16,128,256]{2,1,0:T(8,128)} custom-call(bf16[8,256,256]{2,1,0:T(8,128)(2,1)S(1)} %get-tuple-element.7.zt, f32[16,128,256]{2,1,0:T(8,128)S(1)} %get-tuple-element.8.state), custom_call_target="tpu_custom_call" | custom-call | tf_op jit(solution)/shard_map/pallas_call | solution.py:473

commit v4 on v3

--- a/solution.py
+++ b/solution.py
@@ -17,7 +17,8 @@
 CELLS = 128
 U = TX + 16
 W = TY + 128
-G = 14
+G = 6
+DEPTH = (G + 2) * C
 BF = jnp.bfloat16
 F32 = jnp.float32
 MESH = pl.DeviceIdType.MESH
@@ -26,6 +27,8 @@
 
 STEPS = ((-1, 0), (1, 0), (0, -1), (0, 1), (-1, -1), (-1, 1), (1, -1), (1, 1))
 OPPOSITE = (1, 0, 3, 2, 7, 6, 5, 4)
+ROW_ORDER = (10, 6, 9, 7, 8, 11, 5, 12, 4, 13, 3, 14, 2, 15, 1)
+COL_ORDER = (6, 2, 5, 3, 4, 7, 1)
 
 
 def iota2(shape, dim):
@@ -63,6 +66,25 @@
 def normed(coarse):
     mean = jnp.mean(coarse * coarse, axis=-1, keepdims=True)
     return (coarse * lax.rsqrt(mean + 1e-06)).astype(BF)
+
+
+def softmax(scores):
+    scores = scores * (E // H) ** (-0.5)
+    top = jnp.max(scores, axis=-1, keepdims=True)
+    powers = jnp.exp(scores - top)
+    return (powers / jnp.sum(powers, axis=-1, keepdims=True)).astype(BF)
+
+
+def packed(cells):
+    parts = cells.reshape(16, 8, E)
+    return (
+        jnp.stack([parts[:, :, :128], parts[:, :, 128:]], axis=1).reshape(256, 128).astype(BF)
+    )
+
+
+def unpacked(rows):
+    parts = rows.astype(F32).reshape(16, 2, 8, 128)
+    return jnp.concatenate([parts[:, 0], parts[:, 1]], axis=-1).reshape(CELLS, E)
 
 
 def attend(cells, w_q, w_k, w_v):
@@ -73,10 +95,7 @@
     query_set = jnp.concatenate(
         [jnp.where(head == h, queries, 0.0).astype(BF) for h in range(H)], axis=0
     )
-    scores = mm(query_set, lookups, NT) * (E // H) ** (-0.5)
-    top = jnp.max(scores, axis=-1, keepdims=True)
-    powers = jnp.exp(scores - top)
-    weights = (powers / jnp.sum(powers, axis=-1, keepdims=True)).astype(BF)
+    weights = softmax(mm(query_set, lookups, NT))
     mixed = jnp.zeros((128, E), F32)
     for h in range(H):
         mixed = mixed + mm(
@@ -90,28 +109,11 @@
     state, zt,
     surf, cp, wst, wp, wu, wq, wqkvo, sw, am, s_ref, bb,
     row_s, col_s, row_r, col_r, corner_r,
-    n0, g0, mix0, m0, n1, g1, mix1, m1,
-    load_sem, halo_send, halo_recv, a2a_send, a2a_recv,
+    g0, k0, v0, n1, g1, mix1, m1,
+    load_sem, halo_send, halo_recv, gather_send, gather_recv, a2a_send, a2a_recv,
 ):
     row = lax.axis_index("row")
     col = lax.axis_index("col")
-
-    loads = []
-
-    def load(src, dst):
-        copy = pltpu.make_async_copy(src, dst, load_sem.at[len(loads)])
-        copy.start()
-        loads.append(copy)
-
-    for i in range(8):
-        load(surface.at[:, pl.ds(16 * i, 16), :], surf.at[:, pl.ds(16 * i, 16), :])
-    for l in range(LAYERS):
-        load(coupling.at[l], cp.at[l, pl.ds(8, TX), pl.ds(0, TY)])
-    load(w_stencil, wst)
-    load(w_patch, wp)
-    for n, w in enumerate((w_query, w_key, w_value, w_out)):
-        load(w, wqkvo.at[n])
-    load(w_unpatch, wu)
 
     row_r[...] = jnp.zeros_like(row_r)
     col_r[...] = jnp.zeros_like(col_r)
@@ -149,17 +151,29 @@
 
         expected = expected + jnp.where(has(step), 1, 0)
 
+    loads = []
+
+    def load(src, dst):
+        copy = pltpu.make_async_copy(src, dst, load_sem.at[len(loads)])
+        copy.start()
+        loads.append(copy)
+
+    for i in range(8):
+        load(surface.at[:, pl.ds(16 * i, 16), :], surf.at[:, pl.ds(16 * i, 16), :])
+    for l in range(LAYERS):
+        load(coupling.at[l], cp.at[l, pl.ds(8, TX), pl.ds(0, TY)])
+    load(w_stencil, wst)
+    load(w_patch, wp)
+    for n, w in enumerate((w_query, w_key, w_value, w_out)):
+        load(w, wqkvo.at[n])
+    load(w_unpatch, wu)
+
     sw[...] = swap_matrix()
 
     for i in range(8):
         loads[i].wait()
-        block = surf[:, 16 * i : 16 * (i + 1), :].reshape(256, TY)
-        high = block.astype(BF)
-        low = (block - high.astype(F32)).astype(BF)
-        turned = mm(sw[...], high)
-        rows = pl.ds((8 + 16 * i) * C, 256)
-        bb[0, rows, 0:TY] = turned.astype(BF)
-        s_ref[rows, 0:TY] = turned + mm(sw[...], low)
+        high = surf[:, 16 * i : 16 * (i + 1), :].reshape(256, TY).astype(BF)
+        bb[0, pl.ds((8 + 16 * i) * C, 256), 0:TY] = mm(sw[...], high).astype(BF)
 
     strip = jnp.zeros((32, 512), F32)
     for k in range(4):
@@ -167,7 +181,7 @@
             strip_select(k, TY, 0, TY - 3), bb[0, pl.ds((8 + 32 * k) * C, 512), 0:TY], NT
         )
     strip = strip.astype(BF)
-    for l in range(LAYERS):
+    for l in range(2):
         loads[8 + l].wait()
     cols = jnp.zeros((32, TX), F32)
     rows_c = jnp.zeros((32, TY), F32)
@@ -212,10 +226,16 @@
             device_id_type=MESH,
         )
 
-    for d in range(8):
+    for d in (4, 5, 6, 7, 2, 3, 0, 1):
         @pl.when(has(STEPS[d]))
         def _():
             halo_copy(d).start()
+
+    for i in range(8):
+        block = surf[:, 16 * i : 16 * (i + 1), :].reshape(256, TY)
+        low = (block - block.astype(BF).astype(F32)).astype(BF)
+        rows = pl.ds((8 + 16 * i) * C, 256)
+        s_ref[rows, 0:TY] = bb[0, rows, 0:TY].astype(F32) + mm(sw[...], low)
 
     s_ref[0:80, 0:TY] = jnp.zeros((80, TY), F32)
     s_ref[139 * 16 : U * 16, 0:TY] = jnp.zeros((80, TY), F32)
@@ -227,10 +247,11 @@
     cp[2, 8 + TX : U, :] = jnp.zeros((8, W), F32)
     cp[2, 8 : 8 + TX, TY:W] = jnp.zeros((TX, 128), F32)
 
+    loads[10].wait()
     loads[11].wait()
-    spread = ones_where((iota2((C, 256), 1) & 15) == iota2((C, 256), 0))
+    spread = ones_where((iota2((C, DEPTH), 1) & 15) == iota2((C, DEPTH), 0))
     tiled = mm(wst[...].astype(BF), spread)
-    band = iota2((C, 256), 1) >> 4
+    band = iota2((C, DEPTH), 1) >> 4
     for l in range(LAYERS):
         for b in range(3):
             pick = [
@@ -244,7 +265,7 @@
                         band == xo + 1, pick[1], jnp.where(band == xo + 2, pick[2], 0.0)
                     ),
                 )
-                am[l, C * xo : C * (xo + 1), 256 * b : 256 * (b + 1)] = block.astype(BF)
+                am[l, C * xo : C * (xo + 1), DEPTH * b : DEPTH * (b + 1)] = block.astype(BF)
 
     loads[12].wait()
     for p in range(PATCH):
@@ -289,34 +310,40 @@
 
     for l in range(LAYERS):
         src, dst = l % 2, (l + 1) % 2
-        wide = W if l < LAYERS - 1 else TY
-        for k in range(10):
-            u = 6 + l + G * k
-            count = G if k < 9 else 6
-            depth = (count + 2) * C
-            window = bb[src, (u - 1) * C : (u - 1) * C + depth, :]
-            shifted = (
-                jnp.concatenate([window[:, W - 1 :], window[:, : wide - 1]], axis=1),
-                window[:, :wide],
-                jnp.concatenate([window[:, 1:], window[:, :1]], axis=1)[:, :wide],
+
+        def shifted(u):
+            window = bb[src, (u - 1) * C : (u - 1) * C + DEPTH, :]
+            return jnp.concatenate(
+                [
+                    jnp.concatenate([window[:, W - 1 :], window[:, : W - 1]], axis=1),
+                    window,
+                    jnp.concatenate([window[:, 1:], window[:, :1]], axis=1),
+                ],
+                axis=0,
             )
-            if count == G:
-                mix = mm(am[l], jnp.concatenate(shifted, axis=0))
-            else:
-                mix = sum(
-                    mm(am[l, 0 : count * C, 256 * b : 256 * b + depth], shifted[b])
-                    for b in range(3)
-                )
-            gain = jnp.tanh(mix)
-            for x in range(count):
+
+        def update(u, gain, lanes):
+            for x in range(G):
                 if u + x > 137 - l:
                     continue
                 rows = slice((u + x) * C, (u + x + 1) * C)
-                new = s_ref[rows, :wide] + cp[l, u + x : u + x + 1, :wide] * (
+                new = s_ref[rows, lanes] + cp[l, u + x : u + x + 1, lanes] * (
                     gain[C * x : C * (x + 1)]
                 )
-                s_ref[rows, :wide] = new
-                bb[dst, rows, :wide] = new.astype(BF)
+                s_ref[rows, lanes] = new
+                bb[dst, rows, lanes] = new.astype(BF)
+
+        for pair in range(11):
+            starts = [6 + l + G * (2 * pair + n) for n in range(2)]
+            windows = [shifted(u) for u in starts]
+            for u, window in zip(starts, windows):
+                update(u, jnp.tanh(mm(am[l], window[:, :TY])), slice(0, TY))
+            if l < LAYERS - 1:
+                edges = jnp.tanh(
+                    mm(am[l], jnp.concatenate([window[:, TY:] for window in windows], axis=1))
+                )
+                for n, u in enumerate(starts):
+                    update(u, edges[:, 128 * n : 128 * (n + 1)], slice(TY, W))
 
     last = LAYERS % 2
     for i in range(8):
@@ -326,40 +353,40 @@
     for q in range(PATCH):
         coarse = coarse + mm(zt[:, 16 * q : 16 * (q + 1), :].reshape(CELLS, 256), wq[q])
 
-    def a2a(phase, src, dst, peer_slot, peer, rows, me):
+    def a2a(phase, src, dst, d):
+        rows = pl.ds(16 * d, 16)
         return pltpu.make_async_remote_copy(
-            src_ref=src.at[pl.ds(pl.multiple_of(peer_slot * rows, rows), rows)],
-            dst_ref=dst.at[pl.ds(pl.multiple_of(me * rows, rows), rows)],
-            send_sem=a2a_send.at[phase, peer_slot],
-            recv_sem=a2a_recv.at[phase, me],
-            device_id=peer,
+            src_ref=src.at[rows],
+            dst_ref=dst.at[rows],
+            send_sem=a2a_send.at[phase, d],
+            recv_sem=a2a_recv.at[phase],
+            device_id=(lax.rem(row + (d if phase == 0 else NR - d), NR), col),
             device_id_type=MESH,
         )
 
-    def exchange(phase, src, dst, axis, between=None):
-        size, rows, me = (NC, 16, col) if axis == "col" else (NR, 8, row)
-
-        def peer_of(d):
-            slot = lax.rem(me + d, size)
-            return slot, ((row, slot) if axis == "col" else (slot, col))
-
-        for d in range(1, size):
-            slot, peer = peer_of(d)
-            a2a(phase, src, dst, slot, peer, rows, me).start()
-        own = pl.ds(pl.multiple_of(me * rows, rows), rows)
-        dst[own, :] = src[own, :]
-        if between is not None:
-            between()
-        for d in range(1, size):
-            slot, peer = peer_of(d)
-            a2a(phase, src, dst, me, peer, rows, slot).wait_recv()
-
-        def sent():
-            for d in range(1, size):
-                slot, peer = peer_of(d)
-                a2a(phase, src, dst, slot, peer, rows, me).wait_send()
-
-        return sent
+    def exchange(phase, src, dst):
+        for d in ROW_ORDER:
+            a2a(phase, src, dst, d).start()
+        dst[0:16, :] = src[0:16, :]
+        rest = pl.ds(16, 16 * (NR - 1))
+        pltpu.make_async_remote_copy(
+            src_ref=src.at[rest],
+            dst_ref=dst.at[rest],
+            send_sem=a2a_send.at[phase, 1],
+            recv_sem=a2a_recv.at[phase],
+            device_id=(lax.rem(row + 1, NR), col),
+            device_id_type=MESH,
+        ).wait_recv()
+
+    def gather(d):
+        return pltpu.make_async_remote_copy(
+            src_ref=g0.at[0],
+            dst_ref=g0.at[d],
+            send_sem=gather_send.at[d],
+            recv_sem=gather_recv.at[d],
+            device_id=(row, lax.rem(col + d, NC)),
+            device_id_type=MESH,
+        )
 
     def state_back():
         for i in range(8):
@@ -375,20 +402,48 @@
             turned = mm(sw[...], wu[:, 256 * c : 256 * (c + 1)], NT).astype(BF)
             wq[:, C * c : C * (c + 1), :] = turned.reshape(PATCH, C, E)
 
-    n0[...] = normed(coarse)
-    sent0 = exchange(0, n0, g0, "col", state_back)
-    mix0[...] = attend(g0[...], wqkvo[0, 0], wqkvo[1, 0], wqkvo[2, 0]).astype(BF)
-    sent1 = exchange(1, mix0, m0, "col", unpatch_weights)
-    coarse = coarse + mm(m0[...], wqkvo[3, 0])
+    g0[0] = normed(coarse)
+    for d in COL_ORDER:
+        gather(d).start()
+    head = iota2((16, E), 1) >> 5
+    queries = mm(g0[0], wqkvo[0, 0])
+    query_sets = [
+        jnp.concatenate(
+            [
+                jnp.where(head == h, queries[16 * i : 16 * (i + 1)], 0.0).astype(BF)
+                for h in range(H)
+            ],
+            axis=0,
+        )
+        for i in range(8)
+    ]
+    state_back()
+    unpatch_weights()
+    for d in range(NC):
+        if d > 0:
+            gather(d).wait_recv()
+        k0[d] = mm(g0[d], wqkvo[1, 0]).astype(BF)
+        v0[d] = mm(g0[d], wqkvo[2, 0]).astype(BF)
+    mixed = []
+    for i in range(8):
+        rows = slice(16 * i, 16 * (i + 1))
+        weights = softmax(mm(query_sets[i], k0[:, rows, :].reshape(128, E), NT))
+        whole = mm(weights, v0[:, rows, :].reshape(128, E))
+        mixed.append(
+            sum(jnp.where(head == h, whole[16 * h : 16 * (h + 1)], 0.0) for h in range(H))
+        )
+    coarse = coarse + mm(jnp.concatenate(mixed, axis=0).astype(BF), wqkvo[3, 0])
 
     r = iota2((CELLS, CELLS), 0)
     k = iota2((CELLS, CELLS), 1)
-    turn = ones_where(k == (r & 7) * 16 + (r >> 3))
-    n1[...] = mm(turn, normed(coarse))
-    sent2 = exchange(2, n1, g1, "row")
-    mix1[...] = attend(g1[...].astype(BF), wqkvo[0, 1], wqkvo[1, 1], wqkvo[2, 1])
-    sent3 = exchange(3, mix1, m1, "row")
-    back = mm(turn, m1[...].astype(BF), TN).astype(BF)
+    turn = ones_where(k == (r & 7) * 16 + (((r >> 3) + row) & 15))
+    n1[...] = packed(mm(turn, normed(coarse)))
+    exchange(0, n1, g1)
+    mix1[...] = packed(
+        attend(unpacked(g1[...]).astype(BF), wqkvo[0, 1], wqkvo[1, 1], wqkvo[2, 1])
+    )
+    exchange(1, mix1, m1)
+    back = mm(turn, unpacked(m1[...]).astype(BF), TN).astype(BF)
     coarse = coarse + mm(back, wqkvo[3, 1])
     coarse = coarse.astype(BF)
     for q in range(PATCH):
@@ -399,8 +454,11 @@
         def _():
             halo_copy(d).wait_send()
 
-    for sent in (sent0, sent1, sent2, sent3):
-        sent()
+    for d in COL_ORDER:
+        gather(d).wait_send()
+    for d in ROW_ORDER:
+        a2a(0, n1, g1, d).wait_send()
+        a2a(1, mix1, m1, d).wait_send()
 
 
 def add_kernel(zt, state, out, swap, held, store_sem):
@@ -434,7 +492,7 @@
             pltpu.VMEM((PATCH, 256, E), BF),
             pltpu.VMEM((4, 2, E, E), BF),
             pltpu.VMEM((256, 256), BF),
-            pltpu.VMEM((LAYERS, G * C, 768), BF),
+            pltpu.VMEM((LAYERS, G * C, 3 * DEPTH), BF),
             pltpu.VMEM((U * C, W), F32),
             pltpu.VMEM((2, U * C, W), BF),
             pltpu.VMEM((2, 64, TY), BF),
@@ -442,19 +500,20 @@
             pltpu.VMEM((2, 64, TY), BF),
             pltpu.VMEM((2, 16, 768), BF),
             pltpu.VMEM((4, 16, 256), BF),
-            pltpu.VMEM((CELLS, E), BF),
-            pltpu.VMEM((CELLS, E), BF),
-            pltpu.VMEM((CELLS, E), BF),
-            pltpu.VMEM((CELLS, E), BF),
-            pltpu.VMEM((CELLS, E), F32),
-            pltpu.VMEM((CELLS, E), F32),
-            pltpu.VMEM((CELLS, E), F32),
-            pltpu.VMEM((CELLS, E), F32),
+            pltpu.VMEM((NC, CELLS, E), BF),
+            pltpu.VMEM((NC, CELLS, E), BF),
+            pltpu.VMEM((NC, CELLS, E), BF),
+            pltpu.VMEM((256, 128), BF),
+            pltpu.VMEM((256, 128), BF),
+            pltpu.VMEM((256, 128), BF),
+            pltpu.VMEM((256, 128), BF),
             pltpu.SemaphoreType.DMA((18,)),
             pltpu.SemaphoreType.DMA((8,)),
             pltpu.SemaphoreType.DMA((8,)),
-            pltpu.SemaphoreType.DMA((4, NR)),
-            pltpu.SemaphoreType.DMA((4, NR)),
+            pltpu.SemaphoreType.DMA((NC,)),
+            pltpu.SemaphoreType.DMA((NC,)),
+            pltpu.SemaphoreType.DMA((2, NR)),
+            pltpu.SemaphoreType.DMA((2,)),
         ],
         compiler_params=pltpu.CompilerParams(
             collective_id=0, has_side_effects=True, vmem_limit_bytes=60 * 1024 * 1024

time: 42.8 us -> 41.7 us (0.974)
  Pallas kernels: 42.7 us -> 41.6 us
    pallas_call x1, Pallas kernels: 41 us -> 40 us  [on_device(): pl.pallas_call(main_kernel, out_shape=(pltpu.VMEM((C, TX, TY), F32), pltp...]
where the time goes in v4:
time: 41.7 us; the launch traced here: 41.6 us
  Pallas kernels  41.6 us (100%)
    pallas_call x1, Pallas kernels, on_device(): pl.pallas_call(main_kernel, out_shape=(pltpu.VMEM((C, TX, TY), F32), pltp...  40 us
    pallas_call x1, Pallas kernels, on_device(): pl.pallas_call(add_kernel, out_shape=jax.ShapeDtypeStruct((C, TX, TY), F3...  1.63 us

profile of v4, /device:TPU:1, one launch (start us, length us, event | category | flops | bytes accessed | tf_op | source)
XLA Modules:
  0.0 41.6 jit_solution(3111025269244548063)
XLA Ops:
  0.0 40.0 %shard_map.91 = (f32[16,128,256]{2,1,0:T(8,128)S(1)}, bf16[8,256,256]{2,1,0:T(8,128)(2,1)S(1)}) custom-call(f32[16,128,256]{2,1,0:T(8,128)} %surface.1, f32[3,128,256]{2,1,0:T(8,128)} %coupling.1, f32[432,16]{1,0:T(8,128)} %bitcast.3, bf16[16,16,16,256]{3,2,1,0:T(8,128)(2,1)} %bitcast.2, bf16[2,256,256]{2,1,0:T(8,128)(2,1)} %w_query.1, ...), custom_call_target="tpu_custom_call" | custom-call | tf_op jit(solution)/shard_map/pallas_call | solution.py:481
  40.0 1.6 %shard_map.92 = f32[16,128,256]{2,1,0:T(8,128)} custom-call(bf16[8,256,256]{2,1,0:T(8,128)(2,1)S(1)} %get-tuple-element.7.zt, f32[16,128,256]{2,1,0:T(8,128)S(1)} %get-tuple-element.8.state), custom_call_target="tpu_custom_call" | custom-call | tf_op jit(solution)/shard_map/pallas_call | solution.py:532

commit v5 on v4

--- a/solution.py
+++ b/solution.py
@@ -27,8 +27,9 @@
 
 STEPS = ((-1, 0), (1, 0), (0, -1), (0, 1), (-1, -1), (-1, 1), (1, -1), (1, 1))
 OPPOSITE = (1, 0, 3, 2, 7, 6, 5, 4)
-ROW_ORDER = (10, 6, 9, 7, 8, 11, 5, 12, 4, 13, 3, 14, 2, 15, 1)
-COL_ORDER = (6, 2, 5, 3, 4, 7, 1)
+ROW_ORDER = (10, 11, 8, 9, 14, 15, 12, 13, 6, 7, 4, 5, 2, 3, 1)
+COL_ORDER = (6, 5, 7, 2, 4, 1, 3)
+GATHER_ORDER = (2, 1, 3, 4, 6, 5, 7)
 
 
 def iota2(shape, dim):
@@ -73,6 +74,10 @@
     top = jnp.max(scores, axis=-1, keepdims=True)
     powers = jnp.exp(scores - top)
     return (powers / jnp.sum(powers, axis=-1, keepdims=True)).astype(BF)
+
+
+def flipped(bits, d):
+    return sum(((1 - bit) if (d >> n) & 1 else bit) * (1 << n) for n, bit in enumerate(bits))
 
 
 def packed(cells):
@@ -114,6 +119,8 @@
 ):
     row = lax.axis_index("row")
     col = lax.axis_index("col")
+    row_bits = [lax.rem(lax.div(row, 1 << n), 2) for n in range(4)]
+    col_bits = [lax.rem(lax.div(col, 1 << n), 2) for n in range(3)]
 
     row_r[...] = jnp.zeros_like(row_r)
     col_r[...] = jnp.zeros_like(col_r)
@@ -308,50 +315,76 @@
         cp[l, 0:8, TY:W] = mm(above[:, 128:256], strip_place(l), TN)[TX - 8 : TX]
         cp[l, 8 + TX : U, TY:W] = mm(below[:, 0:128], strip_place(l), TN)[0:8]
 
-    for l in range(LAYERS):
-        src, dst = l % 2, (l + 1) % 2
-
-        def shifted(u):
-            window = bb[src, (u - 1) * C : (u - 1) * C + DEPTH, :]
-            return jnp.concatenate(
-                [
-                    jnp.concatenate([window[:, W - 1 :], window[:, : W - 1]], axis=1),
-                    window,
-                    jnp.concatenate([window[:, 1:], window[:, :1]], axis=1),
-                ],
-                axis=0,
+    def gather(half, d):
+        cells = pl.ds(64 * half, 64)
+        return pltpu.make_async_remote_copy(
+            src_ref=g0.at[0, cells],
+            dst_ref=g0.at[d, cells],
+            send_sem=gather_send.at[half, d],
+            recv_sem=gather_recv.at[half, d],
+            device_id=(row, flipped(col_bits, d)),
+            device_id_type=MESH,
+        )
+
+    def shifted(src, u):
+        window = bb[src, (u - 1) * C : (u - 1) * C + DEPTH, :]
+        return jnp.concatenate(
+            [
+                jnp.concatenate([window[:, W - 1 :], window[:, : W - 1]], axis=1),
+                window,
+                jnp.concatenate([window[:, 1:], window[:, :1]], axis=1),
+            ],
+            axis=0,
+        )
+
+    def update(l, u, gain, lanes):
+        for x in range(G):
+            if u + x > 137 - l:
+                continue
+            rows = slice((u + x) * C, (u + x + 1) * C)
+            new = s_ref[rows, lanes] + cp[l, u + x : u + x + 1, lanes] * (
+                gain[C * x : C * (x + 1)]
             )
-
-        def update(u, gain, lanes):
-            for x in range(G):
-                if u + x > 137 - l:
-                    continue
-                rows = slice((u + x) * C, (u + x + 1) * C)
-                new = s_ref[rows, lanes] + cp[l, u + x : u + x + 1, lanes] * (
-                    gain[C * x : C * (x + 1)]
-                )
-                s_ref[rows, lanes] = new
-                bb[dst, rows, lanes] = new.astype(BF)
-
-        for pair in range(11):
-            starts = [6 + l + G * (2 * pair + n) for n in range(2)]
-            windows = [shifted(u) for u in starts]
-            for u, window in zip(starts, windows):
-                update(u, jnp.tanh(mm(am[l], window[:, :TY])), slice(0, TY))
-            if l < LAYERS - 1:
-                edges = jnp.tanh(
-                    mm(am[l], jnp.concatenate([window[:, TY:] for window in windows], axis=1))
-                )
-                for n, u in enumerate(starts):
-                    update(u, edges[:, 128 * n : 128 * (n + 1)], slice(TY, W))
+            s_ref[rows, lanes] = new
+            bb[(l + 1) % 2, rows, lanes] = new.astype(BF)
+
+    def advance(l, pair):
+        starts = [6 + l + G * (2 * pair + n) for n in range(2)]
+        windows = [shifted(l % 2, u) for u in starts]
+        for u, window in zip(starts, windows):
+            update(l, u, jnp.tanh(mm(am[l], window[:, :TY])), slice(0, TY))
+        if l < LAYERS - 1:
+            edges = jnp.tanh(
+                mm(am[l], jnp.concatenate([window[:, TY:] for window in windows], axis=1))
+            )
+            for n, u in enumerate(starts):
+                update(l, u, edges[:, 128 * n : 128 * (n + 1)], slice(TY, W))
 
     last = LAYERS % 2
-    for i in range(8):
-        block = bb[last, pl.ds((8 + 16 * i) * C, 256), 0:TY]
-        zt[i] = mm(sw[...], block, NT).astype(BF)
-    coarse = jnp.zeros((CELLS, E), F32)
-    for q in range(PATCH):
-        coarse = coarse + mm(zt[:, 16 * q : 16 * (q + 1), :].reshape(CELLS, 256), wq[q])
+
+    def patch(half):
+        for i in range(4 * half, 4 * half + 4):
+            block = bb[last, pl.ds((8 + 16 * i) * C, 256), 0:TY]
+            zt[i] = mm(sw[...], block, NT).astype(BF)
+        part = jnp.zeros((CELLS // 2, E), F32)
+        for q in range(PATCH):
+            block = zt[4 * half : 4 * half + 4, 16 * q : 16 * (q + 1), :]
+            part = part + mm(block.reshape(CELLS // 2, 256), wq[q])
+        g0[0, 64 * half : 64 * half + 64, :] = normed(part)
+        for d in COL_ORDER:
+            gather(half, d).start()
+        return part
+
+    parts = []
+    for step in range(11 + 2 * (LAYERS - 1)):
+        for l in range(LAYERS):
+            pair = step - 2 * l
+            if 0 <= pair < 11:
+                advance(l, pair)
+                if l == LAYERS - 1 and pair == 5:
+                    parts.append(patch(0))
+    parts.append(patch(1))
+    coarse = jnp.concatenate(parts, axis=0)
 
     def a2a(phase, src, dst, d):
         rows = pl.ds(16 * d, 16)
@@ -360,7 +393,7 @@
             dst_ref=dst.at[rows],
             send_sem=a2a_send.at[phase, d],
             recv_sem=a2a_recv.at[phase],
-            device_id=(lax.rem(row + (d if phase == 0 else NR - d), NR), col),
+            device_id=(flipped(row_bits, d), col),
             device_id_type=MESH,
         )
 
@@ -374,19 +407,9 @@
             dst_ref=dst.at[rest],
             send_sem=a2a_send.at[phase, 1],
             recv_sem=a2a_recv.at[phase],
-            device_id=(lax.rem(row + 1, NR), col),
+            device_id=(flipped(row_bits, 1), col),
             device_id_type=MESH,
         ).wait_recv()
-
-    def gather(d):
-        return pltpu.make_async_remote_copy(
-            src_ref=g0.at[0],
-            dst_ref=g0.at[d],
-            send_sem=gather_send.at[d],
-            recv_sem=gather_recv.at[d],
-            device_id=(row, lax.rem(col + d, NC)),
-            device_id_type=MESH,
-        )
 
     def state_back():
         for i in range(8):
@@ -402,41 +425,33 @@
             turned = mm(sw[...], wu[:, 256 * c : 256 * (c + 1)], NT).astype(BF)
             wq[:, C * c : C * (c + 1), :] = turned.reshape(PATCH, C, E)
 
-    g0[0] = normed(coarse)
-    for d in COL_ORDER:
-        gather(d).start()
+    state_back()
     head = iota2((16, E), 1) >> 5
     queries = mm(g0[0], wqkvo[0, 0])
-    query_sets = [
-        jnp.concatenate(
-            [
-                jnp.where(head == h, queries[16 * i : 16 * (i + 1)], 0.0).astype(BF)
-                for h in range(H)
-            ],
-            axis=0,
-        )
-        for i in range(8)
-    ]
-    state_back()
     unpatch_weights()
-    for d in range(NC):
-        if d > 0:
-            gather(d).wait_recv()
-        k0[d] = mm(g0[d], wqkvo[1, 0]).astype(BF)
-        v0[d] = mm(g0[d], wqkvo[2, 0]).astype(BF)
     mixed = []
-    for i in range(8):
-        rows = slice(16 * i, 16 * (i + 1))
-        weights = softmax(mm(query_sets[i], k0[:, rows, :].reshape(128, E), NT))
-        whole = mm(weights, v0[:, rows, :].reshape(128, E))
-        mixed.append(
-            sum(jnp.where(head == h, whole[16 * h : 16 * (h + 1)], 0.0) for h in range(H))
-        )
+    for half in range(2):
+        cells = slice(64 * half, 64 * half + 64)
+        for d in (0,) + GATHER_ORDER:
+            if d > 0:
+                gather(half, d).wait_recv()
+            k0[d, cells, :] = mm(g0[d, cells, :], wqkvo[1, 0]).astype(BF)
+            v0[d, cells, :] = mm(g0[d, cells, :], wqkvo[2, 0]).astype(BF)
+        for i in range(4 * half, 4 * half + 4):
+            rows = slice(16 * i, 16 * (i + 1))
+            query_set = jnp.concatenate(
+                [jnp.where(head == h, queries[rows], 0.0).astype(BF) for h in range(H)], axis=0
+            )
+            weights = softmax(mm(query_set, k0[:, rows, :].reshape(128, E), NT))
+            whole = mm(weights, v0[:, rows, :].reshape(128, E))
+            mixed.append(
+                sum(jnp.where(head == h, whole[16 * h : 16 * (h + 1)], 0.0) for h in range(H))
+            )
     coarse = coarse + mm(jnp.concatenate(mixed, axis=0).astype(BF), wqkvo[3, 0])
 
     r = iota2((CELLS, CELLS), 0)
     k = iota2((CELLS, CELLS), 1)
-    turn = ones_where(k == (r & 7) * 16 + (((r >> 3) + row) & 15))
+    turn = ones_where(k == (r & 7) * 16 + ((r >> 3) ^ row))
     n1[...] = packed(mm(turn, normed(coarse)))
     exchange(0, n1, g1)
     mix1[...] = packed(
@@ -454,8 +469,9 @@
         def _():
             halo_copy(d).wait_send()
 
-    for d in COL_ORDER:
-        gather(d).wait_send()
+    for half in range(2):
+        for d in COL_ORDER:
+            gather(half, d).wait_send()
     for d in ROW_ORDER:
         a2a(0, n1, g1, d).wait_send()
         a2a(1, mix1, m1, d).wait_send()
@@ -510,8 +526,8 @@
             pltpu.SemaphoreType.DMA((18,)),
             pltpu.SemaphoreType.DMA((8,)),
             pltpu.SemaphoreType.DMA((8,)),
-            pltpu.SemaphoreType.DMA((NC,)),
-            pltpu.SemaphoreType.DMA((NC,)),
+            pltpu.SemaphoreType.DMA((2, NC)),
+            pltpu.SemaphoreType.DMA((2, NC)),
             pltpu.SemaphoreType.DMA((2, NR)),
             pltpu.SemaphoreType.DMA((2,)),
         ],

time: 41.7 us -> 40.2 us (0.964)
  Pallas kernels: 41.6 us -> 40.1 us
    pallas_call x1, Pallas kernels: 40 us -> 38.5 us  [on_device(): pl.pallas_call(main_kernel, out_shape=(pltpu.VMEM((C, TX, TY), F32), pltp...]
where the time goes in v5:
time: 40.2 us; the launch traced here: 40.1 us
  Pallas kernels  40.1 us (100%)
    pallas_call x1, Pallas kernels, on_device(): pl.pallas_call(main_kernel, out_shape=(pltpu.VMEM((C, TX, TY), F32), pltp...  38.5 us
    pallas_call x1, Pallas kernels, on_device(): pl.pallas_call(add_kernel, out_shape=jax.ShapeDtypeStruct((C, TX, TY), F3...  1.63 us

profile of v5, /device:TPU:1, one launch (start us, length us, event | category | flops | bytes accessed | tf_op | source)
XLA Modules:
  0.0 40.1 jit_solution(18176861682188706746)
XLA Ops:
  0.0 38.5 %shard_map.91 = (f32[16,128,256]{2,1,0:T(8,128)S(1)}, bf16[8,256,256]{2,1,0:T(8,128)(2,1)S(1)}) custom-call(f32[16,128,256]{2,1,0:T(8,128)} %surface.1, f32[3,128,256]{2,1,0:T(8,128)} %coupling.1, f32[432,16]{1,0:T(8,128)} %bitcast.3, bf16[16,16,16,256]{3,2,1,0:T(8,128)(2,1)} %bitcast.2, bf16[2,256,256]{2,1,0:T(8,128)(2,1)} %w_query.1, ...), custom_call_target="tpu_custom_call" | custom-call | tf_op jit(solution)/shard_map/pallas_call | solution.py:497
  38.5 1.6 %shard_map.92 = f32[16,128,256]{2,1,0:T(8,128)} custom-call(bf16[8,256,256]{2,1,0:T(8,128)(2,1)S(1)} %get-tuple-element.7.zt, f32[16,128,256]{2,1,0:T(8,128)S(1)} %get-tuple-element.8.state), custom_call_target="tpu_custom_call" | custom-call | tf_op jit(solution)/shard_map/pallas_call | solution.py:548

commit v6 on v5

--- a/solution.py
+++ b/solution.py
@@ -69,11 +69,9 @@
     return (coarse * lax.rsqrt(mean + 1e-06)).astype(BF)
 
 
-def softmax(scores):
+def powers_of(scores):
     scores = scores * (E // H) ** (-0.5)
-    top = jnp.max(scores, axis=-1, keepdims=True)
-    powers = jnp.exp(scores - top)
-    return (powers / jnp.sum(powers, axis=-1, keepdims=True)).astype(BF)
+    return jnp.exp(scores - jnp.max(scores, axis=-1, keepdims=True)).astype(BF)
 
 
 def flipped(bits, d):
@@ -92,27 +90,34 @@
     return jnp.concatenate([parts[:, 0], parts[:, 1]], axis=-1).reshape(CELLS, E)
 
 
-def attend(cells, w_q, w_k, w_v):
-    queries = mm(cells, w_q)
-    lookups = mm(cells, w_k).astype(BF)
+def own_lanes(head, stacked):
+    return sum(jnp.where(head == h, stacked[16 * h : 16 * (h + 1)], 0.0) for h in range(H))
+
+
+def attend(cells, w_q, w_k_turned, w_v):
+    queries = mm(cells, w_q).astype(BF)
+    lookups = mm(w_k_turned, cells, NT)
     values = mm(cells, w_v)
     head = iota2((128, E), 1) >> 5
-    query_set = jnp.concatenate(
-        [jnp.where(head == h, queries, 0.0).astype(BF) for h in range(H)], axis=0
-    )
-    weights = softmax(mm(query_set, lookups, NT))
-    mixed = jnp.zeros((128, E), F32)
-    for h in range(H):
-        mixed = mixed + mm(
-            weights[128 * h : 128 * (h + 1)], jnp.where(head == h, values, 0.0).astype(BF)
-        )
-    return mixed
+    channel_head = iota2((E, 128), 0) >> 5
+    lookup_set = jnp.concatenate(
+        [jnp.where(channel_head == h, lookups, 0.0).astype(BF) for h in range(H)], axis=1
+    )
+    scores = mm(queries, lookup_set)
+    powers = jnp.concatenate(
+        [powers_of(scores[:, 128 * h : 128 * (h + 1)]) for h in range(H)], axis=1
+    )
+    value_set = jnp.concatenate(
+        [jnp.where(head == h, values, 0.0).astype(BF) for h in range(H)], axis=0
+    )
+    own_head = jnp.concatenate([ones_where(head == h) for h in range(H)], axis=0)
+    return mm(powers, value_set) / mm(powers, own_head)
 
 
 def main_kernel(
     surface, coupling, w_stencil, w_patch, w_query, w_key, w_value, w_out, w_unpatch,
     state, zt,
-    surf, cp, wst, wp, wu, wq, wqkvo, sw, am, s_ref, bb,
+    surf, cp, wst, wp, wu, wq, wqkvo, wkt, sw, am, s_ref, bb,
     row_s, col_s, row_r, col_r, corner_r,
     g0, k0, v0, n1, g1, mix1, m1,
     load_sem, halo_send, halo_recv, gather_send, gather_recv, a2a_send, a2a_recv,
@@ -140,16 +145,8 @@
         return ok
 
     barrier = pltpu.get_barrier_semaphore()
-    for d in range(1, NC):
-        pl.semaphore_signal(
-            barrier, inc=1, device_id=(row, lax.rem(col + d, NC)), device_id_type=MESH
-        )
-    for d in range(1, NR):
-        pl.semaphore_signal(
-            barrier, inc=1, device_id=(lax.rem(row + d, NR), col), device_id_type=MESH
-        )
-    expected = jnp.int32(NC - 1 + NR - 1)
-    for step in STEPS[4:]:
+    expected = jnp.int32(0)
+    for step in STEPS[4:] + STEPS[:4]:
         @pl.when(has(step))
         def _():
             pl.semaphore_signal(
@@ -157,7 +154,6 @@
             )
 
         expected = expected + jnp.where(has(step), 1, 0)
-
     loads = []
 
     def load(src, dst):
@@ -170,17 +166,28 @@
     for l in range(LAYERS):
         load(coupling.at[l], cp.at[l, pl.ds(8, TX), pl.ds(0, TY)])
     load(w_stencil, wst)
+
+    for d in COL_ORDER:
+        pl.semaphore_signal(
+            barrier, inc=1, device_id=(row, flipped(col_bits, d)), device_id_type=MESH
+        )
+    for d in ROW_ORDER:
+        pl.semaphore_signal(
+            barrier, inc=1, device_id=(flipped(row_bits, d), col), device_id_type=MESH
+        )
+    expected = expected + (NC - 1 + NR - 1)
+
+    sw[...] = swap_matrix()
+
+    for i in range(8):
+        loads[i].wait()
+        high = surf[:, 16 * i : 16 * (i + 1), :].reshape(256, TY).astype(BF)
+        bb[0, pl.ds((8 + 16 * i) * C, 256), 0:TY] = mm(sw[...], high).astype(BF)
+
     load(w_patch, wp)
     for n, w in enumerate((w_query, w_key, w_value, w_out)):
         load(w, wqkvo.at[n])
     load(w_unpatch, wu)
-
-    sw[...] = swap_matrix()
-
-    for i in range(8):
-        loads[i].wait()
-        high = surf[:, 16 * i : 16 * (i + 1), :].reshape(256, TY).astype(BF)
-        bb[0, pl.ds((8 + 16 * i) * C, 256), 0:TY] = mm(sw[...], high).astype(BF)
 
     strip = jnp.zeros((32, 512), F32)
     for k in range(4):
@@ -315,14 +322,14 @@
         cp[l, 0:8, TY:W] = mm(above[:, 128:256], strip_place(l), TN)[TX - 8 : TX]
         cp[l, 8 + TX : U, TY:W] = mm(below[:, 0:128], strip_place(l), TN)[0:8]
 
-    def gather(half, d):
+    def gather(half, d, peer=None):
         cells = pl.ds(64 * half, 64)
         return pltpu.make_async_remote_copy(
             src_ref=g0.at[0, cells],
             dst_ref=g0.at[d, cells],
             send_sem=gather_send.at[half, d],
             recv_sem=gather_recv.at[half, d],
-            device_id=(row, flipped(col_bits, d)),
+            device_id=(row, flipped(col_bits, d) if peer is None else peer),
             device_id_type=MESH,
         )
 
@@ -371,8 +378,11 @@
             block = zt[4 * half : 4 * half + 4, 16 * q : 16 * (q + 1), :]
             part = part + mm(block.reshape(CELLS // 2, 256), wq[q])
         g0[0, 64 * half : 64 * half + 64, :] = normed(part)
-        for d in COL_ORDER:
-            gather(half, d).start()
+        for target in range(NC):
+            @pl.when(col != target)
+            def _():
+                gather(half, flipped(col_bits, target), target).start()
+
         return part
 
     parts = []
@@ -420,6 +430,8 @@
             state[:, 16 * i : 16 * (i + 1), :] = turned.reshape(C, 16, TY)
 
     def unpatch_weights():
+        one = ones_where(iota2((E, E), 0) == iota2((E, E), 1))
+        wkt[...] = mm(wqkvo[1, 1], one, TN).astype(BF)
         loads[17].wait()
         for c in range(C):
             turned = mm(sw[...], wu[:, 256 * c : 256 * (c + 1)], NT).astype(BF)
@@ -442,11 +454,10 @@
             query_set = jnp.concatenate(
                 [jnp.where(head == h, queries[rows], 0.0).astype(BF) for h in range(H)], axis=0
             )
-            weights = softmax(mm(query_set, k0[:, rows, :].reshape(128, E), NT))
-            whole = mm(weights, v0[:, rows, :].reshape(128, E))
-            mixed.append(
-                sum(jnp.where(head == h, whole[16 * h : 16 * (h + 1)], 0.0) for h in range(H))
-            )
+            powers = powers_of(mm(query_set, k0[:, rows, :].reshape(128, E), NT))
+            whole = mm(powers, v0[:, rows, :].reshape(128, E))
+            total = mm(powers, jnp.ones((128, E), BF))
+            mixed.append(own_lanes(head, whole) / own_lanes(head, total))
     coarse = coarse + mm(jnp.concatenate(mixed, axis=0).astype(BF), wqkvo[3, 0])
 
     r = iota2((CELLS, CELLS), 0)
@@ -455,7 +466,7 @@
     n1[...] = packed(mm(turn, normed(coarse)))
     exchange(0, n1, g1)
     mix1[...] = packed(
-        attend(unpacked(g1[...]).astype(BF), wqkvo[0, 1], wqkvo[1, 1], wqkvo[2, 1])
+        attend(unpacked(g1[...]).astype(BF), wqkvo[0, 1], wkt[...], wqkvo[2, 1])
     )
     exchange(1, mix1, m1)
     back = mm(turn, unpacked(m1[...]).astype(BF), TN).astype(BF)
@@ -507,6 +518,7 @@
             pltpu.VMEM((E, C * 256), BF),
             pltpu.VMEM((PATCH, 256, E), BF),
             pltpu.VMEM((4, 2, E, E), BF),
+            pltpu.VMEM((E, E), BF),
             pltpu.VMEM((256, 256), BF),
             pltpu.VMEM((LAYERS, G * C, 3 * DEPTH), BF),
             pltpu.VMEM((U * C, W), F32),

time: 40.2 us -> 39.6 us (0.985)
  Pallas kernels: 40.1 us -> 39.5 us
    pallas_call x1, Pallas kernels: 38.5 us -> 37.9 us  [on_device(): pl.pallas_call(main_kernel, out_shape=(pltpu.VMEM((C, TX, TY), F32), pltp...]
where the time goes in v6:
time: 39.6 us; the launch traced here: 39.5 us
  Pallas kernels  39.5 us (100%)
    pallas_call x1, Pallas kernels, on_device(): pl.pallas_call(main_kernel, out_shape=(pltpu.VMEM((C, TX, TY), F32), pltp...  37.9 us
    pallas_call x1, Pallas kernels, on_device(): pl.pallas_call(add_kernel, out_shape=jax.ShapeDtypeStruct((C, TX, TY), F3...  1.63 us

profile of v6, /device:TPU:1, one launch (start us, length us, event | category | flops | bytes accessed | tf_op | source)
XLA Modules:
  0.0 39.5 jit_solution(4127401173266990119)
XLA Ops:
  0.0 37.9 %shard_map.91 = (f32[16,128,256]{2,1,0:T(8,128)S(1)}, bf16[8,256,256]{2,1,0:T(8,128)(2,1)S(1)}) custom-call(f32[16,128,256]{2,1,0:T(8,128)} %surface.1, f32[3,128,256]{2,1,0:T(8,128)} %coupling.1, f32[432,16]{1,0:T(8,128)} %bitcast.3, bf16[16,16,16,256]{3,2,1,0:T(8,128)(2,1)} %bitcast.2, bf16[2,256,256]{2,1,0:T(8,128)(2,1)} %w_query.1, ...), custom_call_target="tpu_custom_call" | custom-call | tf_op jit(solution)/shard_map/pallas_call | solution.py:508
  37.9 1.6 %shard_map.92 = f32[16,128,256]{2,1,0:T(8,128)} custom-call(bf16[8,256,256]{2,1,0:T(8,128)(2,1)S(1)} %get-tuple-element.7.zt, f32[16,128,256]{2,1,0:T(8,128)S(1)} %get-tuple-element.8.state), custom_call_target="tpu_custom_call" | custom-call | tf_op jit(solution)/shard_map/pallas_call | solution.py:560

commit v7 on v6

--- a/solution.py
+++ b/solution.py
@@ -30,6 +30,7 @@
 ROW_ORDER = (10, 11, 8, 9, 14, 15, 12, 13, 6, 7, 4, 5, 2, 3, 1)
 COL_ORDER = (6, 5, 7, 2, 4, 1, 3)
 GATHER_ORDER = (2, 1, 3, 4, 6, 5, 7)
+PARTS = ((0, 3), (3, 8))
 
 
 def iota2(shape, dim):
@@ -323,7 +324,8 @@
         cp[l, 8 + TX : U, TY:W] = mm(below[:, 0:128], strip_place(l), TN)[0:8]
 
     def gather(half, d, peer=None):
-        cells = pl.ds(64 * half, 64)
+        first, end = PARTS[half]
+        cells = pl.ds(16 * first, 16 * (end - first))
         return pltpu.make_async_remote_copy(
             src_ref=g0.at[0, cells],
             dst_ref=g0.at[d, cells],
@@ -370,14 +372,16 @@
     last = LAYERS % 2
 
     def patch(half):
-        for i in range(4 * half, 4 * half + 4):
+        first, end = PARTS[half]
+        count = 16 * (end - first)
+        for i in range(first, end):
             block = bb[last, pl.ds((8 + 16 * i) * C, 256), 0:TY]
             zt[i] = mm(sw[...], block, NT).astype(BF)
-        part = jnp.zeros((CELLS // 2, E), F32)
+        part = jnp.zeros((count, E), F32)
         for q in range(PATCH):
-            block = zt[4 * half : 4 * half + 4, 16 * q : 16 * (q + 1), :]
-            part = part + mm(block.reshape(CELLS // 2, 256), wq[q])
-        g0[0, 64 * half : 64 * half + 64, :] = normed(part)
+            block = zt[first:end, 16 * q : 16 * (q + 1), :]
+            part = part + mm(block.reshape(count, 256), wq[q])
+        g0[0, 16 * first : 16 * end, :] = normed(part)
         for target in range(NC):
             @pl.when(col != target)
             def _():
@@ -391,7 +395,7 @@
             pair = step - 2 * l
             if 0 <= pair < 11:
                 advance(l, pair)
-                if l == LAYERS - 1 and pair == 5:
+                if l == LAYERS - 1 and pair == 3:
                     parts.append(patch(0))
     parts.append(patch(1))
     coarse = jnp.concatenate(parts, axis=0)
@@ -407,10 +411,11 @@
             device_id_type=MESH,
         )
 
-    def exchange(phase, src, dst):
+    def exchange(phase, src, dst, meanwhile):
         for d in ROW_ORDER:
             a2a(phase, src, dst, d).start()
         dst[0:16, :] = src[0:16, :]
+        meanwhile()
         rest = pl.ds(16, 16 * (NR - 1))
         pltpu.make_async_remote_copy(
             src_ref=src.at[rest],
@@ -437,19 +442,27 @@
             turned = mm(sw[...], wu[:, 256 * c : 256 * (c + 1)], NT).astype(BF)
             wq[:, C * c : C * (c + 1), :] = turned.reshape(PATCH, C, E)
 
-    state_back()
+    def before_columns():
+        state_back()
+        unpatch_weights()
+
+    def before_unpatch():
+        one = ones_where(iota2((E, E), 0) == iota2((E, E), 1))
+        for q in range(PATCH):
+            wq[q] = mm(wq[q], one, TN).astype(BF)
+
     head = iota2((16, E), 1) >> 5
     queries = mm(g0[0], wqkvo[0, 0])
-    unpatch_weights()
     mixed = []
     for half in range(2):
-        cells = slice(64 * half, 64 * half + 64)
+        first, end = PARTS[half]
+        cells = slice(16 * first, 16 * end)
         for d in (0,) + GATHER_ORDER:
             if d > 0:
                 gather(half, d).wait_recv()
             k0[d, cells, :] = mm(g0[d, cells, :], wqkvo[1, 0]).astype(BF)
             v0[d, cells, :] = mm(g0[d, cells, :], wqkvo[2, 0]).astype(BF)
-        for i in range(4 * half, 4 * half + 4):
+        for i in range(first, end):
             rows = slice(16 * i, 16 * (i + 1))
             query_set = jnp.concatenate(
                 [jnp.where(head == h, queries[rows], 0.0).astype(BF) for h in range(H)], axis=0
@@ -464,16 +477,16 @@
     k = iota2((CELLS, CELLS), 1)
     turn = ones_where(k == (r & 7) * 16 + ((r >> 3) ^ row))
     n1[...] = packed(mm(turn, normed(coarse)))
-    exchange(0, n1, g1)
+    exchange(0, n1, g1, before_columns)
     mix1[...] = packed(
         attend(unpacked(g1[...]).astype(BF), wqkvo[0, 1], wkt[...], wqkvo[2, 1])
     )
-    exchange(1, mix1, m1)
+    exchange(1, mix1, m1, before_unpatch)
     back = mm(turn, unpacked(m1[...]).astype(BF), TN).astype(BF)
     coarse = coarse + mm(back, wqkvo[3, 1])
     coarse = coarse.astype(BF)
     for q in range(PATCH):
-        cells = mm(coarse, wq[q], NT).astype(BF)
+        cells = mm(coarse, wq[q]).astype(BF)
         zt[:, 16 * q : 16 * (q + 1), :] = cells.reshape(8, 16, 256)
     for d in range(8):
         @pl.when(has(STEPS[d]))

time: 39.6 us -> 38.9 us (0.982)
  Pallas kernels: 39.5 us -> 38.8 us
    pallas_call x1, Pallas kernels: 37.9 us -> 37.1 us  [on_device(): pl.pallas_call(main_kernel, out_shape=(pltpu.VMEM((C, TX, TY), F32), pltp...]
where the time goes in v7:
time: 38.9 us; the launch traced here: 38.8 us
  Pallas kernels  38.8 us (100%)
    pallas_call x1, Pallas kernels, on_device(): pl.pallas_call(main_kernel, out_shape=(pltpu.VMEM((C, TX, TY), F32), pltp...  37.1 us
    pallas_call x1, Pallas kernels, on_device(): pl.pallas_call(add_kernel, out_shape=jax.ShapeDtypeStruct((C, TX, TY), F3...  1.63 us

profile of v7, /device:TPU:1, one launch (start us, length us, event | category | flops | bytes accessed | tf_op | source)
XLA Modules:
  0.0 38.8 jit_solution(17232250796831542337)
XLA Ops:
  0.0 37.1 %shard_map.91 = (f32[16,128,256]{2,1,0:T(8,128)S(1)}, bf16[8,256,256]{2,1,0:T(8,128)(2,1)S(1)}) custom-call(f32[16,128,256]{2,1,0:T(8,128)} %surface.1, f32[3,128,256]{2,1,0:T(8,128)} %coupling.1, f32[432,16]{1,0:T(8,128)} %bitcast.3, bf16[16,16,16,256]{3,2,1,0:T(8,128)(2,1)} %bitcast.2, bf16[2,256,256]{2,1,0:T(8,128)(2,1)} %w_query.1, ...), custom_call_target="tpu_custom_call" | custom-call | tf_op jit(solution)/shard_map/pallas_call | solution.py:521
  37.1 1.6 %shard_map.92 = f32[16,128,256]{2,1,0:T(8,128)} custom-call(bf16[8,256,256]{2,1,0:T(8,128)(2,1)S(1)} %get-tuple-element.7.zt, f32[16,128,256]{2,1,0:T(8,128)S(1)} %get-tuple-element.8.state), custom_call_target="tpu_custom_call" | custom-call | tf_op jit(solution)/shard_map/pallas_call | solution.py:573

commit v8 on v7

--- a/solution.py
+++ b/solution.py
@@ -30,7 +30,7 @@
 ROW_ORDER = (10, 11, 8, 9, 14, 15, 12, 13, 6, 7, 4, 5, 2, 3, 1)
 COL_ORDER = (6, 5, 7, 2, 4, 1, 3)
 GATHER_ORDER = (2, 1, 3, 4, 6, 5, 7)
-PARTS = ((0, 3), (3, 8))
+PARTS = ((0, 2), (2, 8))
 
 
 def iota2(shape, dim):
@@ -395,7 +395,7 @@
             pair = step - 2 * l
             if 0 <= pair < 11:
                 advance(l, pair)
-                if l == LAYERS - 1 and pair == 3:
+                if l == LAYERS - 1 and pair == 2:
                     parts.append(patch(0))
     parts.append(patch(1))
     coarse = jnp.concatenate(parts, axis=0)

time: 38.9 us -> 39.7 us (1.021)
  Pallas kernels: 38.8 us -> 39.6 us
    pallas_call x1, Pallas kernels: 37.1 us -> 37.9 us  [on_device(): pl.pallas_call(main_kernel, out_shape=(pltpu.VMEM((C, TX, TY), F32), pltp...]
where the time goes in v8:
time: 39.7 us; the launch traced here: 39.6 us
  Pallas kernels  39.6 us (100%)
    pallas_call x1, Pallas kernels, on_device(): pl.pallas_call(main_kernel, out_shape=(pltpu.VMEM((C, TX, TY), F32), pltp...  37.9 us
    pallas_call x1, Pallas kernels, on_device(): pl.pallas_call(add_kernel, out_shape=jax.ShapeDtypeStruct((C, TX, TY), F3...  1.63 us

profile of v8, /device:TPU:1, one launch (start us, length us, event | category | flops | bytes accessed | tf_op | source)
XLA Modules:
  0.0 39.6 jit_solution(4166938596694444648)
XLA Ops:
  0.0 37.9 %shard_map.91 = (f32[16,128,256]{2,1,0:T(8,128)S(1)}, bf16[8,256,256]{2,1,0:T(8,128)(2,1)S(1)}) custom-call(f32[16,128,256]{2,1,0:T(8,128)} %surface.1, f32[3,128,256]{2,1,0:T(8,128)} %coupling.1, f32[432,16]{1,0:T(8,128)} %bitcast.3, bf16[16,16,16,256]{3,2,1,0:T(8,128)(2,1)} %bitcast.2, bf16[2,256,256]{2,1,0:T(8,128)(2,1)} %w_query.1, ...), custom_call_target="tpu_custom_call" | custom-call | tf_op jit(solution)/shard_map/pallas_call | solution.py:521
  37.9 1.6 %shard_map.92 = f32[16,128,256]{2,1,0:T(8,128)} custom-call(bf16[8,256,256]{2,1,0:T(8,128)(2,1)S(1)} %get-tuple-element.7.zt, f32[16,128,256]{2,1,0:T(8,128)S(1)} %get-tuple-element.8.state), custom_call_target="tpu_custom_call" | custom-call | tf_op jit(solution)/shard_map/pallas_call | solution.py:573
